TPU v7x, 32 devices: a whole 2x2x4 slice. The times are simulated.
32 devices in a mesh: section: 2 (over core), dp: 4 (over z), tensor: 4 (over y, x).
Axes of the slice: x: 2, y: 2, z: 4, core: 2. Of those that a mesh axis runs over, the one named last changes fastest.
Arguments:
- inputs: bfloat16 [8, 1088, 768], P('dp', 'tensor'), may hold values from -6 to 6
- cotangent: bfloat16 [8, 1088, 768], P('dp', 'tensor'), may hold values from -6 to 6
- w_qkv: bfloat16 [2, 3, 768, 768], P('section', None, None, 'tensor'), may hold values from -0.21875 to 0.21875
- w_out: bfloat16 [2, 768, 768], P('section', 'tensor'), may hold values from -1.75 to 1.75
- w_up: bfloat16 [2, 768, 3072], P('section', None, 'tensor'), may hold values from -0.21875 to 0.21875
- w_down: bfloat16 [2, 3072, 768], P('section', 'tensor'), may hold values from -0.109375 to 0.109375
- gains: float32 [2, 2, 768], P('section'), may hold values from 0.5 to 1.5
- image_sizes: int32 [8, 2], P('dp'), may hold values from 12 to 24, as said below
- lengths: int32 [8], P('dp'), may hold values from 5 to 512, as said below
- shifts: int32 [2], replicated, may hold values from 1 to 11
Outputs:
- ends: bfloat16 [2, 8, 1088, 768], P('section', 'dp', 'tensor')
- grad_qkv: float32 [2, 3, 768, 768], P('section', None, 'dp', 'tensor')
- grad_out: float32 [2, 768, 768], P('section', 'tensor', 'dp')
- grad_up: float32 [2, 768, 3072], P('section', 'dp', 'tensor')
- grad_down: float32 [2, 3072, 768], P('section', ('tensor', 'dp'))
- grad_gains: float32 [2, 2, 768], P('section', None, ('dp', 'tensor'))
Inputs may be any that keep to these rules, and one draw needn't show every extreme that they name: `image_sizes`: one image of each draw covers the whole grid. `lengths`: one image of each draw fills all 512 answer slots.
All inputs are finite; a program needn't handle non-finite values.
Results may differ from a plain program's by a relative error of at most 0.025.
Values may be sent and summed in bfloat16 or wider, within the bound.
A program may use at most 192 MiB of HBM per device.

v0:
```python
import jax
import jax.numpy as jnp
from jax import lax
from jax.sharding import PartitionSpec as P

HD = 64
WIN = 12
GRID = 24
QL = 512


epsilon = 1e-05
masked_score = -1000000000.0


def on_whole(slab, axis, dim, apply):
    everything = lax.all_gather(slab, axis, axis=dim, tiled=True)
    return apply(everything, jnp.int32(0))


def shifted(block, axis, distance):
    devices = range(lax.axis_size(axis))
    route = [(i - distance, i) for i in devices if i - distance in devices]
    return lax.ppermute(block, axis, route)


def allowed_pairs(image_size, answer_length, offsets):
    patches = GRID * GRID
    tokens = jnp.arange(patches + QL, dtype=jnp.int32)
    is_patch = tokens < patches
    grid_row = tokens // GRID
    grid_col = tokens % GRID
    live_patch = is_patch & (grid_row < image_size[0]) & (grid_col < image_size[1])
    live_answer = jnp.logical_not(is_patch) & (tokens - patches < answer_length)
    window_row = (grid_row + offsets[0]) // WIN
    window_col = (grid_col + offsets[1]) // WIN
    same_window = (window_row[:, None] == window_row[None, :]) & (
        window_col[:, None] == window_col[None, :]
    )
    from_patch = is_patch[:, None] & live_patch[None, :] & same_window
    earlier = live_answer[None, :] & (tokens[None, :] < tokens[:, None])
    from_answer = jnp.logical_not(is_patch)[:, None] & (live_patch[None, :] | earlier)
    return from_patch | from_answer | (tokens[:, None] == tokens[None, :])


def normalize(values, gain):
    centered = values - jnp.mean(values, axis=-1, keepdims=True)
    inverse = lax.rsqrt(jnp.mean(centered * centered, axis=-1, keepdims=True) + epsilon)
    normed = centered * inverse
    return (normed * gain, normed, inverse)


def normalize_back(grad_scaled, normed, inverse, gain):
    grad_normed = grad_scaled * gain
    grad_values = inverse * (
        grad_normed
        - jnp.mean(grad_normed, axis=-1, keepdims=True)
        - normed * jnp.mean(grad_normed * normed, axis=-1, keepdims=True)
    )
    return (grad_values, jnp.sum(grad_scaled * normed, axis=0))


def gather_project(normed_low, project):
    return on_whole(normed_low, "tensor", 0, lambda segment, anchor: (segment, project(segment)))


def gather_back(grad_low, project):
    return on_whole(grad_low, "tensor", 0, lambda segment, anchor: (segment, project(segment)))


def project_scatter(left_low, weight, row_count):

    def term(anchor, amount):
        return jnp.dot(left_low, weight, preferred_element_type=jnp.float32)

    return lax.psum_scatter(
        term(jnp.int32(0), row_count * lax.axis_size("tensor")).astype(jnp.bfloat16),
        "tensor",
        scatter_dimension=0,
        tiled=True,
    ).astype(jnp.float32)


def scatter_back(term, row_count):
    return lax.psum_scatter(
        term(jnp.int32(0), row_count * lax.axis_size("tensor")).astype(jnp.bfloat16),
        "tensor",
        scatter_dimension=0,
        tiled=True,
    ).astype(jnp.float32)


def send_forward(rows):
    return shifted(rows, "section", 1)


def send_backward(rows):
    return shifted(rows, "section", -1)


def attention_scores(query, key_heads, allowed):
    scores = jnp.einsum(
        "qhe,khe->hqk", query, key_heads, preferred_element_type=jnp.float32
    ) * HD ** (-0.5)
    return jnp.where(allowed[None], scores, masked_score)


def section_forward(values, weights, allowed):
    qkv_weight, out_weight, up_weight, down_weight, gain_pair = weights
    row_count = values.shape[0]
    first, normed_one, inverse_one = normalize(values, gain_pair[0])
    first_full, projected = gather_project(
        first.astype(jnp.bfloat16),
        lambda segment: jnp.einsum(
            "sd,jde->sje", segment, qkv_weight, preferred_element_type=jnp.float32
        ),
    )
    projected = projected.astype(jnp.bfloat16)
    token_count = projected.shape[0]
    local_width = projected.shape[2]
    head_parts = projected.reshape(token_count, 3, local_width // HD, HD)
    scores = attention_scores(head_parts[:, 0], head_parts[:, 1], allowed)
    row_max = jnp.max(scores, axis=-1, keepdims=True)
    expos = jnp.exp(scores - row_max)
    totals = jnp.sum(expos, axis=-1, keepdims=True)
    probs = expos / totals
    log_total = row_max + jnp.log(totals)
    mixed = (
        jnp.einsum(
            "hqk,khe->qhe",
            probs.astype(jnp.bfloat16),
            head_parts[:, 2],
            preferred_element_type=jnp.float32,
        )
        .astype(jnp.bfloat16)
        .reshape(token_count, local_width)
    )
    after_attn = values + project_scatter(mixed, out_weight, row_count)
    second, normed_two, inverse_two = normalize(after_attn, gain_pair[1])
    second_full, hidden = gather_project(
        second.astype(jnp.bfloat16),
        lambda segment: jnp.dot(segment, up_weight, preferred_element_type=jnp.float32),
    )
    acted = jax.nn.gelu(hidden, approximate=False).astype(jnp.bfloat16)
    output = after_attn + project_scatter(acted, down_weight, row_count)
    saved = (
        first_full,
        projected,
        log_total,
        mixed,
        normed_one,
        inverse_one,
        normed_two,
        inverse_two,
        second_full,
        hidden,
    )
    return (output, saved)


def section_backward(grad_output, saved, weights, allowed):
    qkv_weight, out_weight, up_weight, down_weight, gain_pair = weights
    (
        first_full,
        projected,
        log_total,
        mixed,
        normed_one,
        inverse_one,
        normed_two,
        inverse_two,
        second_full,
        hidden,
    ) = saved
    row_count = grad_output.shape[0]
    token_count = projected.shape[0]
    local_width = projected.shape[2]
    grad_branch_full, grad_acted = gather_back(
        grad_output.astype(jnp.bfloat16),
        lambda segment: jnp.einsum(
            "sd,fd->sf", segment, down_weight, preferred_element_type=jnp.float32
        ),
    )
    acted, gelu_pull = jax.vjp(lambda inner: jax.nn.gelu(inner, approximate=False), hidden)
    grad_hidden = gelu_pull(grad_acted)[0].astype(jnp.bfloat16)

    def second_term(anchor, amount):
        return jnp.einsum("sf,df->sd", grad_hidden, up_weight, preferred_element_type=jnp.float32)

    grad_second = scatter_back(second_term, row_count)
    grad_norm_two, gain_grad_two = normalize_back(
        grad_second, normed_two, inverse_two, gain_pair[1]
    )
    grad_after = grad_output + grad_norm_two
    grad_attn_full, grad_mixed = gather_back(
        grad_after.astype(jnp.bfloat16),
        lambda segment: jnp.einsum(
            "sd,cd->sc", segment, out_weight, preferred_element_type=jnp.float32
        ),
    )
    grad_mixed = grad_mixed.astype(jnp.bfloat16).reshape(token_count, local_width // HD, HD)
    head_parts = projected.reshape(token_count, 3, local_width // HD, HD)
    scores = attention_scores(head_parts[:, 0], head_parts[:, 1], allowed)
    probs = jnp.exp(scores - log_total)
    grad_probs = jnp.einsum(
        "qhe,khe->hqk", grad_mixed, head_parts[:, 2], preferred_element_type=jnp.float32
    )
    inner_sum = jnp.sum(grad_probs * probs, axis=-1, keepdims=True)
    grad_scores = (probs * (grad_probs - inner_sum)).astype(jnp.bfloat16)
    grad_query = jnp.einsum(
        "hqk,khe->qhe", grad_scores, head_parts[:, 1], preferred_element_type=jnp.float32
    ) * HD ** (-0.5)
    grad_keys = jnp.einsum(
        "hqk,qhe->khe", grad_scores, head_parts[:, 0], preferred_element_type=jnp.float32
    ) * HD ** (-0.5)
    grad_value = jnp.einsum(
        "hqk,qhe->khe", probs.astype(jnp.bfloat16), grad_mixed, preferred_element_type=jnp.float32
    )
    grad_projected = jnp.stack([grad_query, grad_keys, grad_value], axis=1).reshape(
        token_count, 3, local_width
    )
    grad_projected = grad_projected.astype(jnp.bfloat16)

    def first_term(anchor, amount):
        return jnp.einsum(
            "sje,jde->sd", grad_projected, qkv_weight, preferred_element_type=jnp.float32
        )

    grad_first = scatter_back(first_term, row_count)
    grad_norm_one, gain_grad_one = normalize_back(grad_first, normed_one, inverse_one, gain_pair[0])
    grad_values = grad_after + grad_norm_one
    materials = (grad_branch_full, grad_hidden, grad_attn_full, grad_projected)
    return (grad_values, materials, jnp.stack([gain_grad_one, gain_grad_two]))


def weight_terms(saved, materials):
    (
        first_full,
        projected,
        log_total,
        mixed,
        normed_one,
        inverse_one,
        normed_two,
        inverse_two,
        second_full,
        hidden,
    ) = saved
    grad_branch_full, grad_hidden, grad_attn_full, grad_projected = materials
    acted = jax.nn.gelu(hidden, approximate=False).astype(jnp.bfloat16)
    grad_down_local = jnp.einsum(
        "sf,sd->fd", acted, grad_branch_full, preferred_element_type=jnp.float32
    )
    grad_up_local = jnp.einsum(
        "sd,sf->df", second_full, grad_hidden, preferred_element_type=jnp.float32
    )
    grad_out_local = jnp.einsum(
        "sc,sd->cd", mixed, grad_attn_full, preferred_element_type=jnp.float32
    )
    grad_qkv_local = jnp.einsum(
        "sd,sje->jde", first_full, grad_projected, preferred_element_type=jnp.float32
    )
    return (grad_qkv_local, grad_out_local, grad_up_local, grad_down_local)


def add_weights(totals, terms, factor):
    masked_terms = tuple((term_item * factor for term_item in terms))
    shares = (
        lax.psum_scatter(
            masked_terms[0].astype(jnp.bfloat16), "dp", scatter_dimension=1, tiled=True
        ).astype(jnp.float32),
        lax.psum_scatter(
            masked_terms[1].astype(jnp.bfloat16), "dp", scatter_dimension=1, tiled=True
        ).astype(jnp.float32),
        lax.psum_scatter(
            masked_terms[2].astype(jnp.bfloat16), "dp", scatter_dimension=0, tiled=True
        ).astype(jnp.float32),
        lax.psum_scatter(
            masked_terms[3].astype(jnp.bfloat16), "dp", scatter_dimension=0, tiled=True
        ).astype(jnp.float32),
    )
    return tuple((earlier + latest for earlier, latest in zip(totals, shares)))


def put_item(buffer, new_item, position, valid):
    current = lax.dynamic_index_in_dim(buffer, position, 0, keepdims=False)
    return lax.dynamic_update_index_in_dim(buffer, jnp.where(valid, new_item, current), position, 0)


def take_item(buffer, position):
    return lax.dynamic_index_in_dim(buffer, position, 0, keepdims=False)


def on_device(inputs, cotangent, w_qkv, w_out, w_up, w_down, gains, image_sizes, lengths, shifts):
    section_index = lax.axis_index("section")
    weights = (w_qkv[0], w_out[0], w_up[0], w_down[0], gains[0])
    micro_count = inputs.shape[0]
    row_count = inputs.shape[1]
    model_width = inputs.shape[2]
    dp_count = lax.axis_size("dp")
    local_width = w_qkv.shape[3]
    local_units = w_up.shape[2]
    offsets = shifts * section_index

    def pattern(position):
        return allowed_pairs(
            lax.dynamic_index_in_dim(image_sizes, position, 0, keepdims=False),
            lax.dynamic_index_in_dim(lengths, position, 0, keepdims=False),
            offsets,
        )

    totals_start = (
        jnp.zeros((3, model_width // dp_count, local_width), jnp.float32),
        jnp.zeros((w_out.shape[1], model_width // dp_count), jnp.float32),
        jnp.zeros((model_width // dp_count, local_units), jnp.float32),
        jnp.zeros((w_down.shape[1] // dp_count, model_width), jnp.float32),
    )
    start_rows = jnp.zeros((row_count, model_width), jnp.bfloat16)
    gain_start = jnp.zeros((2, model_width), jnp.float32)

    def forward_tick(carry, tick_number):
        arrived, results = carry
        micro_index = tick_number - section_index
        position = jnp.clip(micro_index, 0, micro_count - 1)
        is_valid = (micro_index >= 0) & (micro_index < micro_count)
        own_rows = take_item(inputs, position)
        source = jnp.where(section_index == 0, own_rows, arrived).astype(jnp.float32)
        output, saved = section_forward(source, weights, pattern(position))
        outgoing = output.astype(jnp.bfloat16)
        arrived = send_forward(outgoing)
        results = put_item(results, outgoing, position, is_valid & (section_index == 1))
        return ((arrived, results), saved)

    (arrived, results), saved_all = lax.scan(
        forward_tick, (start_rows, jnp.zeros_like(inputs)), jnp.arange(micro_count + 1)
    )

    def backward_tick(carry, tick_number):
        arrived, results, totals, gain_total = carry
        micro_index = tick_number - 1 + section_index
        position = jnp.clip(micro_index, 0, micro_count - 1)
        is_valid = (micro_index >= 0) & (micro_index < micro_count)
        factor = is_valid.astype(jnp.float32)
        saved_tick = jnp.clip(micro_index + section_index, 0, micro_count)
        saved = jax.tree.map(lambda stacked: take_item(stacked, saved_tick), saved_all)
        given = take_item(cotangent, position)
        grad_output = jnp.where(section_index == 1, given, arrived).astype(jnp.float32)
        grad_values, materials, gain_terms = section_backward(
            grad_output, saved, weights, pattern(position)
        )
        outgoing = grad_values.astype(jnp.bfloat16)
        arrived = send_backward(outgoing)
        results = put_item(results, outgoing, position, is_valid & (section_index == 0))
        totals = add_weights(totals, weight_terms(saved, materials), factor)
        gain_total = gain_total + factor * gain_terms
        return ((arrived, results, totals, gain_total), None)

    (arrived, results, totals, gain_total), unused = lax.scan(
        backward_tick, (start_rows, results, totals_start, gain_start), jnp.arange(micro_count + 1)
    )
    gain_share = lax.psum_scatter(gain_total, ("dp", "tensor"), scatter_dimension=1, tiled=True)
    return (
        results[None],
        totals[0][None],
        totals[1][None],
        totals[2][None],
        totals[3][None],
        gain_share[None],
    )


def solution(mesh):
    placed = (
        P("dp", "tensor", None),
        P("dp", "tensor", None),
        P("section", None, None, "tensor"),
        P("section", "tensor", None),
        P("section", None, "tensor"),
        P("section", "tensor", None),
        P("section", None, None),
        P("dp", None),
        P("dp"),
        P(),
    )
    return jax.shard_map(
        on_device,
        mesh=mesh,
        in_specs=placed,
        out_specs=(
            P("section", "dp", "tensor", None),
            P("section", None, "dp", "tensor"),
            P("section", "tensor", "dp"),
            P("section", "dp", "tensor"),
            P("section", ("tensor", "dp"), None),
            P("section", None, ("dp", "tensor")),
        ),
        check_vma=False,
    )
```

profile of v0, /device:TPU:0, one launch (start us, length us, event | category | flops | bytes accessed | tf_op | source)
XLA Modules:
  0.0 1539.2 jit_solution(10072282604642095454)
XLA Ops:
  11.6 564.9 %while.61 = (s32[]{:T(128)}, bf16[272,768]{1,0:T(8,128)(2,1)}, bf16[2,272,768]{2,1,0:T(8,128)(2,1)}, bf16[3,1088,768]{2,1,0:T(8,128)(2,1)}, bf16[3,1088,3,192]{1...) while((s32[]{:T(128)}, bf16[272,768]{1,0:T(8,128)(2,1)}, ...), condition=%wide.region_9.10_spmd, body=%wide.region_0.9_spmd.sunk | while | flops 4867956736 | bytes 143158992 | solution.py:334
  29.0 22.4 %all-gather.5.cloned.1.call-done = bf16[1088,768]{1,0:T(8,128)(2,1)} async-done(((bf16[272,768]{1,0:T(8,128)(2,1)}), bf16[1088,768]{1,0:T(8,128)(2,1)}) %all-gather.5.cloned.1.call-update) | async-done | bytes 1671184 | tf_op jit(solution)/shard_map/while/body/eval_jaxpr/all_gather | solution.py:17
  55.8 8.3 fusion.278
  64.1 7.3 fusion.279
  71.5 8.1 fusion.280
  81.5 31.8 %reduce-scatter.22.cloned.1.call-done = bf16[272,768]{1,0:T(8,128)(2,1)} async-done(((bf16[1088,768]{1,0:T(8,128)(2,1)}), bf16[272,768]{1,0:T(8,128)(2,1)}) %reduce-scatter.22.cloned.1.call-update) | async-done | bytes 417808 | tf_op jit(solution)/shard_map/while/body/eval_jaxpr/reduce_scatter | solution.py:76
  117.8 31.9 %all-gather.7.cloned.1.call-done = bf16[1088,768]{1,0:T(8,128)(2,1)} async-done(((bf16[272,768]{1,0:T(8,128)(2,1)}), bf16[1088,768]{1,0:T(8,128)(2,1)}) %all-gather.7.cloned.1.call-update) | async-done | bytes 1671184 | tf_op jit(solution)/shard_map/while/body/eval_jaxpr/all_gather | solution.py:17
  154.4 9.7 convolution_convert_fusion.9
  172.5 23.5 %reduce-scatter.24.cloned.1.call-done = bf16[272,768]{1,0:T(8,128)(2,1)} async-done(((bf16[1088,768]{1,0:T(8,128)(2,1)}), bf16[272,768]{1,0:T(8,128)(2,1)}) %reduce-scatter.24.cloned.1.call-update) | async-done | bytes 417808 | tf_op jit(solution)/shard_map/while/body/eval_jaxpr/reduce_scatter | solution.py:76
  219.1 19.7 %all-gather.5.cloned.1.call-done = bf16[1088,768]{1,0:T(8,128)(2,1)} async-done(((bf16[272,768]{1,0:T(8,128)(2,1)}), bf16[1088,768]{1,0:T(8,128)(2,1)}) %all-gather.5.cloned.1.call-update) | async-done | bytes 1671184 | tf_op jit(solution)/shard_map/while/body/eval_jaxpr/all_gather | solution.py:17
  243.2 8.3 fusion.278
  251.5 7.3 fusion.279
  258.8 8.1 fusion.280
  268.8 31.8 %reduce-scatter.22.cloned.1.call-done = bf16[272,768]{1,0:T(8,128)(2,1)} async-done(((bf16[1088,768]{1,0:T(8,128)(2,1)}), bf16[272,768]{1,0:T(8,128)(2,1)}) %reduce-scatter.22.cloned.1.call-update) | async-done | bytes 417808 | tf_op jit(solution)/shard_map/while/body/eval_jaxpr/reduce_scatter | solution.py:76
  305.2 31.9 %all-gather.7.cloned.1.call-done = bf16[1088,768]{1,0:T(8,128)(2,1)} async-done(((bf16[272,768]{1,0:T(8,128)(2,1)}), bf16[1088,768]{1,0:T(8,128)(2,1)}) %all-gather.7.cloned.1.call-update) | async-done | bytes 1671184 | tf_op jit(solution)/shard_map/while/body/eval_jaxpr/all_gather | solution.py:17
  341.8 9.7 convolution_convert_fusion.9
  359.9 23.4 %reduce-scatter.24.cloned.1.call-done = bf16[272,768]{1,0:T(8,128)(2,1)} async-done(((bf16[1088,768]{1,0:T(8,128)(2,1)}), bf16[272,768]{1,0:T(8,128)(2,1)}) %reduce-scatter.24.cloned.1.call-update) | async-done | bytes 417808 | tf_op jit(solution)/shard_map/while/body/eval_jaxpr/reduce_scatter | solution.py:76
  406.5 19.7 %all-gather.5.cloned.1.call-done = bf16[1088,768]{1,0:T(8,128)(2,1)} async-done(((bf16[272,768]{1,0:T(8,128)(2,1)}), bf16[1088,768]{1,0:T(8,128)(2,1)}) %all-gather.5.cloned.1.call-update) | async-done | bytes 1671184 | tf_op jit(solution)/shard_map/while/body/eval_jaxpr/all_gather | solution.py:17
  430.5 8.3 fusion.278
  438.8 7.3 fusion.279
  446.1 8.1 fusion.280
  456.1 31.8 %reduce-scatter.22.cloned.1.call-done = bf16[272,768]{1,0:T(8,128)(2,1)} async-done(((bf16[1088,768]{1,0:T(8,128)(2,1)}), bf16[272,768]{1,0:T(8,128)(2,1)}) %reduce-scatter.22.cloned.1.call-update) | async-done | bytes 417808 | tf_op jit(solution)/shard_map/while/body/eval_jaxpr/reduce_scatter | solution.py:76
  492.5 31.9 %all-gather.7.cloned.1.call-done = bf16[1088,768]{1,0:T(8,128)(2,1)} async-done(((bf16[272,768]{1,0:T(8,128)(2,1)}), bf16[1088,768]{1,0:T(8,128)(2,1)}) %all-gather.7.cloned.1.call-update) | async-done | bytes 1671184 | tf_op jit(solution)/shard_map/while/body/eval_jaxpr/all_gather | solution.py:17
  529.2 9.7 convolution_convert_fusion.9
  547.2 23.5 %reduce-scatter.24.cloned.1.call-done = bf16[272,768]{1,0:T(8,128)(2,1)} async-done(((bf16[1088,768]{1,0:T(8,128)(2,1)}), bf16[272,768]{1,0:T(8,128)(2,1)}) %reduce-scatter.24.cloned.1.call-update) | async-done | bytes 417808 | tf_op jit(solution)/shard_map/while/body/eval_jaxpr/reduce_scatter | solution.py:76
  576.5 826.9 %while.62 = (s32[]{:T(128)}, bf16[272,768]{1,0:T(8,128)(2,1)S(1)}, bf16[2,272,768]{2,1,0:T(8,128)(2,1)}, f32[3,192,192]{1,2,0:T(8,128)S(1)}, f32[192,192]{1,0:T(...) while((s32[]{:T(128)}, bf16[272,768]{1,0:T(8,128)(2,1)S(1)}, ...), condition=%wide.region_24.25_spmd.clone, body=%wide.region_10.24_spmd.clone.sunk | while | flops 10101284864 | bytes 317969888 | solution.py:358
  597.9 32.0 %all-gather.9.cloned.1.call-done = bf16[1088,768]{1,0:T(8,128)(2,1)} async-done(((bf16[272,768]{1,0:T(8,128)(2,1)}), bf16[1088,768]{1,0:T(8,128)(2,1)}) %all-gather.9.cloned.1.call-update) | async-done | bytes 1671184 | tf_op jit(solution)/shard_map/while/body/eval_jaxpr/all_gather | solution.py:17
  630.0 11.9 fusion.301
  646.6 31.0 %reduce-scatter.26.cloned.1.call-done = bf16[272,768]{1,0:T(8,128)(2,1)} async-done(((bf16[1088,768]{1,0:T(8,128)(2,1)}), bf16[272,768]{1,0:T(8,128)(2,1)}) %reduce-scatter.26.cloned.1.call-update) | async-done | bytes 417808 | tf_op jit(solution)/shard_map/while/body/eval_jaxpr/reduce_scatter | solution.py:85
  689.1 6.3 multiply_convert_fusion.12
  700.6 7.5 fusion.309
  715.3 14.1 multiply_reduce_fusion.5
  729.4 9.2 multiply_convert_fusion.10
  746.5 8.4 fusion.310
  755.0 5.5 fusion.311
  776.6 19.7 %reduce-scatter.32.cloned.1.call-done = bf16[192,192]{1,0:T(8,128)(2,1)} async-done(((bf16[768,192]{1,0:T(8,128)(2,1)}), bf16[192,192]{1,0:T(8,128)(2,1)}) %reduce-scatter.32.cloned.1.call-update) | async-done | bytes 73744 | tf_op jit(solution)/shard_map/while
  798.0 25.0 %reduce-scatter.30.cloned.1.call-done = bf16[192,576]{1,0:T(8,128)(2,1)} async-done(((bf16[768,576]{1,0:T(8,128)(2,1)}), bf16[192,576]{1,0:T(8,128)(2,1)}) %reduce-scatter.30.cloned.1.call-update) | async-done | bytes 221200 | tf_op jit(solution)/shard_map/while
  824.5 32.1 %reduce-scatter.28.cloned.1.call-done = bf16[272,768]{1,0:T(8,128)(2,1)} async-done(((bf16[1088,768]{1,0:T(8,128)(2,1)}), bf16[272,768]{1,0:T(8,128)(2,1)}) %reduce-scatter.28.cloned.1.call-update) | async-done | bytes 417808 | tf_op jit(solution)/shard_map/while/body/eval_jaxpr/reduce_scatter | solution.py:85
  867.3 32.1 %all-gather.9.cloned.1.call-done = bf16[1088,768]{1,0:T(8,128)(2,1)} async-done(((bf16[272,768]{1,0:T(8,128)(2,1)}), bf16[1088,768]{1,0:T(8,128)(2,1)}) %all-gather.9.cloned.1.call-update) | async-done | bytes 1671184 | tf_op jit(solution)/shard_map/while/body/eval_jaxpr/all_gather | solution.py:17
  899.4 11.9 fusion.301
  916.0 31.0 %reduce-scatter.26.cloned.1.call-done = bf16[272,768]{1,0:T(8,128)(2,1)} async-done(((bf16[1088,768]{1,0:T(8,128)(2,1)}), bf16[272,768]{1,0:T(8,128)(2,1)}) %reduce-scatter.26.cloned.1.call-update) | async-done | bytes 417808 | tf_op jit(solution)/shard_map/while/body/eval_jaxpr/reduce_scatter | solution.py:85
  958.5 6.2 multiply_convert_fusion.12
  970.0 7.5 fusion.309
  984.7 14.1 multiply_reduce_fusion.5
  998.8 9.2 multiply_convert_fusion.10
  1015.9 8.3 fusion.310
  1024.3 5.4 fusion.311
  1046.3 19.6 %reduce-scatter.32.cloned.1.call-done = bf16[192,192]{1,0:T(8,128)(2,1)} async-done(((bf16[768,192]{1,0:T(8,128)(2,1)}), bf16[192,192]{1,0:T(8,128)(2,1)}) %reduce-scatter.32.cloned.1.call-update) | async-done | bytes 73744 | tf_op jit(solution)/shard_map/while
  1067.6 24.8 %reduce-scatter.30.cloned.1.call-done = bf16[192,576]{1,0:T(8,128)(2,1)} async-done(((bf16[768,576]{1,0:T(8,128)(2,1)}), bf16[192,576]{1,0:T(8,128)(2,1)}) %reduce-scatter.30.cloned.1.call-update) | async-done | bytes 221200 | tf_op jit(solution)/shard_map/while
  1093.8 32.2 %reduce-scatter.28.cloned.1.call-done = bf16[272,768]{1,0:T(8,128)(2,1)} async-done(((bf16[1088,768]{1,0:T(8,128)(2,1)}), bf16[272,768]{1,0:T(8,128)(2,1)}) %reduce-scatter.28.cloned.1.call-update) | async-done | bytes 417808 | tf_op jit(solution)/shard_map/while/body/eval_jaxpr/reduce_scatter | solution.py:85
  1136.8 32.1 %all-gather.9.cloned.1.call-done = bf16[1088,768]{1,0:T(8,128)(2,1)} async-done(((bf16[272,768]{1,0:T(8,128)(2,1)}), bf16[1088,768]{1,0:T(8,128)(2,1)}) %all-gather.9.cloned.1.call-update) | async-done | bytes 1671184 | tf_op jit(solution)/shard_map/while/body/eval_jaxpr/all_gather | solution.py:17
  1168.9 11.9 fusion.301
  1185.5 31.0 %reduce-scatter.26.cloned.1.call-done = bf16[272,768]{1,0:T(8,128)(2,1)} async-done(((bf16[1088,768]{1,0:T(8,128)(2,1)}), bf16[272,768]{1,0:T(8,128)(2,1)}) %reduce-scatter.26.cloned.1.call-update) | async-done | bytes 417808 | tf_op jit(solution)/shard_map/while/body/eval_jaxpr/reduce_scatter | solution.py:85
  1228.1 6.3 multiply_convert_fusion.12
  1239.5 7.5 fusion.309
  1254.2 14.1 multiply_reduce_fusion.5
  1268.3 9.2 multiply_convert_fusion.10
  1280.1 5.3 fusion.312
  1285.4 8.3 fusion.310
  1293.8 5.4 fusion.311
  1315.8 19.7 %reduce-scatter.32.cloned.1.call-done = bf16[192,192]{1,0:T(8,128)(2,1)} async-done(((bf16[768,192]{1,0:T(8,128)(2,1)}), bf16[192,192]{1,0:T(8,128)(2,1)}) %reduce-scatter.32.cloned.1.call-update) | async-done | bytes 73744 | tf_op jit(solution)/shard_map/while
  1337.3 25.0 %reduce-scatter.30.cloned.1.call-done = bf16[192,576]{1,0:T(8,128)(2,1)} async-done(((bf16[768,576]{1,0:T(8,128)(2,1)}), bf16[192,576]{1,0:T(8,128)(2,1)}) %reduce-scatter.30.cloned.1.call-update) | async-done | bytes 221200 | tf_op jit(solution)/shard_map/while
  1363.7 32.1 %reduce-scatter.28.cloned.1.call-done = bf16[272,768]{1,0:T(8,128)(2,1)} async-done(((bf16[1088,768]{1,0:T(8,128)(2,1)}), bf16[272,768]{1,0:T(8,128)(2,1)}) %reduce-scatter.28.cloned.1.call-update) | async-done | bytes 417808 | tf_op jit(solution)/shard_map/while/body/eval_jaxpr/reduce_scatter | solution.py:85
  1406.2 124.2 %reduce-scatter.20.cloned.1.call-done = f32[48,2]{1,0:T(8,128)} async-done(((f32[768,2]{1,0:T(8,128)}), f32[48,2]{1,0:T(8,128)}) %reduce-scatter.20.cloned.1.call-update) | async-done | bytes 400
  (567 shorter events, 339.1 us)
Async XLA Ops:
  11.6 564.9 %copy-start.10 = (f32[3,192,192]{1,2,0:T(8,128)S(1)}, f32[3,192,192]{1,2,0:T(8,128)}, u32[]{:S(2)}) copy-start(f32[3,192,192]{1,2,0:T(8,128)} %custom-call) | copy-start | bytes 1327108
  11.6 39.8 %all-gather.5.cloned.1.call-start = ((), (), s32[]{:S(2)}) async-start(), calls=%async_computation.10 | async-start | bytes 2088960 | tf_op jit(solution)/shard_map/while/body/eval_jaxpr/all_gather | solution.py:17
  15.7 148.5 %copy-start.21 = (f32[272]{0:T(512)}, f32[272]{0:T(512)S(1)}, u32[]{:S(2)}) copy-start(f32[272]{0:T(512)S(1)} %add_rsqrt_fusion.4) | copy-start | bytes 3268 | tf_op jit(solution)/shard_map/while
  16.7 96.5 %reduce-scatter.22.cloned.1.call-start = ((), (), s32[]{:S(2)}) async-start(), calls=%async_computation.11 | async-start | bytes 2088960 | tf_op jit(solution)/shard_map/while/body/eval_jaxpr/reduce_scatter | solution.py:76
  79.5 70.2 %copy-start.8 = (bf16[768,768]{1,0:T(8,128)(2,1)S(1)}, bf16[768,768]{1,0:T(8,128)(2,1)}, u32[]{:S(2)}) copy-start(bf16[768,768]{1,0:T(8,128)(2,1)} %get-tuple-element.1712) | copy-start | bytes 3538948 | tf_op jit(solution)/shard_map/while
  81.4 68.3 %all-gather.7.cloned.1.call-start = ((), (), s32[]{:S(2)}) async-start(), calls=%async_computation.12 | async-start | bytes 2088960 | tf_op jit(solution)/shard_map/while/body/eval_jaxpr/all_gather | solution.py:17
  114.4 40.0 %copy-start.20 = (f32[272]{0:T(512)}, f32[272]{0:T(512)S(1)}, u32[]{:S(2)}) copy-start(f32[272]{0:T(512)S(1)} %broadcast_multiply_fusion.13) | copy-start | bytes 3268 | tf_op jit(solution)/shard_map/while
  115.8 38.7 %copy-start.23 = (f32[272]{0:T(512)}, f32[272]{0:T(512)S(1)}, u32[]{:S(2)}) copy-start(f32[272]{0:T(512)S(1)} %add_rsqrt_fusion.5) | copy-start | bytes 3268 | tf_op jit(solution)/shard_map/while
  117.7 78.2 %reduce-scatter.24.cloned.1.call-start = ((), (), s32[]{:S(2)}) async-start(), calls=%async_computation.13 | async-start | bytes 2088960 | tf_op jit(solution)/shard_map/while/body/eval_jaxpr/reduce_scatter | solution.py:76
  198.0 3.8 collective-permute-start
  201.8 37.1 %all-gather.5.cloned.1.call-start = ((), (), s32[]{:S(2)}) async-start(), calls=%async_computation.10 | async-start | bytes 2088960 | tf_op jit(solution)/shard_map/while/body/eval_jaxpr/all_gather | solution.py:17
  205.8 145.7 %copy-start.21 = (f32[272]{0:T(512)}, f32[272]{0:T(512)S(1)}, u32[]{:S(2)}) copy-start(f32[272]{0:T(512)S(1)} %add_rsqrt_fusion.4) | copy-start | bytes 3268 | tf_op jit(solution)/shard_map/while
  206.9 93.7 %reduce-scatter.22.cloned.1.call-start = ((), (), s32[]{:S(2)}) async-start(), calls=%async_computation.11 | async-start | bytes 2088960 | tf_op jit(solution)/shard_map/while/body/eval_jaxpr/reduce_scatter | solution.py:76
  266.9 70.2 %copy-start.8 = (bf16[768,768]{1,0:T(8,128)(2,1)S(1)}, bf16[768,768]{1,0:T(8,128)(2,1)}, u32[]{:S(2)}) copy-start(bf16[768,768]{1,0:T(8,128)(2,1)} %get-tuple-element.1712) | copy-start | bytes 3538948 | tf_op jit(solution)/shard_map/while
  268.8 68.3 %all-gather.7.cloned.1.call-start = ((), (), s32[]{:S(2)}) async-start(), calls=%async_computation.12 | async-start | bytes 2088960 | tf_op jit(solution)/shard_map/while/body/eval_jaxpr/all_gather | solution.py:17
  301.8 40.0 %copy-start.20 = (f32[272]{0:T(512)}, f32[272]{0:T(512)S(1)}, u32[]{:S(2)}) copy-start(f32[272]{0:T(512)S(1)} %broadcast_multiply_fusion.13) | copy-start | bytes 3268 | tf_op jit(solution)/shard_map/while
  303.1 38.7 %copy-start.23 = (f32[272]{0:T(512)}, f32[272]{0:T(512)S(1)}, u32[]{:S(2)}) copy-start(f32[272]{0:T(512)S(1)} %add_rsqrt_fusion.5) | copy-start | bytes 3268 | tf_op jit(solution)/shard_map/while
  305.1 78.2 %reduce-scatter.24.cloned.1.call-start = ((), (), s32[]{:S(2)}) async-start(), calls=%async_computation.13 | async-start | bytes 2088960 | tf_op jit(solution)/shard_map/while/body/eval_jaxpr/reduce_scatter | solution.py:76
  385.3 3.8 collective-permute-start
  389.1 37.1 %all-gather.5.cloned.1.call-start = ((), (), s32[]{:S(2)}) async-start(), calls=%async_computation.10 | async-start | bytes 2088960 | tf_op jit(solution)/shard_map/while/body/eval_jaxpr/all_gather | solution.py:17
  393.2 145.7 %copy-start.21 = (f32[272]{0:T(512)}, f32[272]{0:T(512)S(1)}, u32[]{:S(2)}) copy-start(f32[272]{0:T(512)S(1)} %add_rsqrt_fusion.4) | copy-start | bytes 3268 | tf_op jit(solution)/shard_map/while
  394.2 93.7 %reduce-scatter.22.cloned.1.call-start = ((), (), s32[]{:S(2)}) async-start(), calls=%async_computation.11 | async-start | bytes 2088960 | tf_op jit(solution)/shard_map/while/body/eval_jaxpr/reduce_scatter | solution.py:76
  454.2 70.2 %copy-start.8 = (bf16[768,768]{1,0:T(8,128)(2,1)S(1)}, bf16[768,768]{1,0:T(8,128)(2,1)}, u32[]{:S(2)}) copy-start(bf16[768,768]{1,0:T(8,128)(2,1)} %get-tuple-element.1712) | copy-start | bytes 3538948 | tf_op jit(solution)/shard_map/while
  456.1 68.3 %all-gather.7.cloned.1.call-start = ((), (), s32[]{:S(2)}) async-start(), calls=%async_computation.12 | async-start | bytes 2088960 | tf_op jit(solution)/shard_map/while/body/eval_jaxpr/all_gather | solution.py:17
  489.1 40.0 %copy-start.20 = (f32[272]{0:T(512)}, f32[272]{0:T(512)S(1)}, u32[]{:S(2)}) copy-start(f32[272]{0:T(512)S(1)} %broadcast_multiply_fusion.13) | copy-start | bytes 3268 | tf_op jit(solution)/shard_map/while
  490.4 38.7 %copy-start.23 = (f32[272]{0:T(512)}, f32[272]{0:T(512)S(1)}, u32[]{:S(2)}) copy-start(f32[272]{0:T(512)S(1)} %add_rsqrt_fusion.5) | copy-start | bytes 3268 | tf_op jit(solution)/shard_map/while
  492.4 78.3 %reduce-scatter.24.cloned.1.call-start = ((), (), s32[]{:S(2)}) async-start(), calls=%async_computation.13 | async-start | bytes 2088960 | tf_op jit(solution)/shard_map/while/body/eval_jaxpr/reduce_scatter | solution.py:76
  572.7 3.8 collective-permute-start
  594.7 35.2 %all-gather.9.cloned.1.call-start = ((), (), s32[]{:S(2)}) async-start(), calls=%async_computation.14 | async-start | bytes 2088960 | tf_op jit(solution)/shard_map/while/body/eval_jaxpr/all_gather | solution.py:17
  597.9 79.7 %reduce-scatter.26.cloned.1.call-start = ((), (), s32[]{:S(2)}) async-start(), calls=%async_computation.15 | async-start | bytes 2088960 | tf_op jit(solution)/shard_map/while/body/eval_jaxpr/reduce_scatter | solution.py:85
  643.0 36.0 %copy-start.2 = (bf16[272,768]{1,0:T(8,128)(2,1)S(1)}, bf16[272,768]{1,0:T(8,128)(2,1)}, u32[]{:S(2)}) copy-start(bf16[272,768]{1,0:T(8,128)(2,1)} %bitcast_select_fusion.6) | copy-start | bytes 1253380 | tf_op jit(solution)/shard_map/while
  645.8 36.1 %copy-start.29 = (s32[2,2]{1,0:T(2,128)S(1)}, s32[2,2]{1,0:T(2,128)}, u32[]{:S(2)}) copy-start(s32[2,2]{1,0:T(2,128)} %get-tuple-element.1808) | copy-start | bytes 52 | tf_op jit(solution)/shard_map/while
  645.8 67.3 %all-gather.11.cloned.1.call-start = ((), (), s32[]{:S(2)}) async-start(), calls=%async_computation.16 | async-start | bytes 2088960 | tf_op jit(solution)/shard_map/while/body/eval_jaxpr/all_gather | solution.py:17
  681.1 91.3 %reduce-scatter.36.cloned.1.call-start = ((), (), s32[]{:S(2)}) async-start(), calls=%async_computation.21 | async-start | bytes 1474560 | tf_op jit(solution)/shard_map/while/body/eval_jaxpr/reduce_scatter | solution.py:278
  695.4 79.3 %reduce-scatter.34.cloned.1.call-start = ((), (), s32[]{:S(2)}) async-start(), calls=%async_computation.20 | async-start | bytes 1474560 | tf_op jit(solution)/shard_map/while/body/eval_jaxpr/reduce_scatter | solution.py:275
  712.4 83.9 %reduce-scatter.32.cloned.1.call-start = ((), (), s32[]{:S(2)}) async-start(), calls=%async_computation.19 | async-start | bytes 491520 | tf_op jit(solution)/shard_map/while
  754.9 68.2 %reduce-scatter.30.cloned.1.call-start = ((), (), s32[]{:S(2)}) async-start(), calls=%async_computation.18 | async-start | bytes 1228800 | tf_op jit(solution)/shard_map/while
  767.3 89.2 %reduce-scatter.28.cloned.1.call-start = ((), (), s32[]{:S(2)}) async-start(), calls=%async_computation.17 | async-start | bytes 2088960 | tf_op jit(solution)/shard_map/while/body/eval_jaxpr/reduce_scatter | solution.py:85
  772.4 85.8 %copy-start.3 = (bf16[272,768]{1,0:T(8,128)(2,1)S(1)}, bf16[272,768]{1,0:T(8,128)(2,1)}, u32[]{:S(2)}) copy-start(bf16[272,768]{1,0:T(8,128)(2,1)} %reduce-scatter.26.cloned.1.call-done) | copy-start | bytes 1253380 | tf_op jit(solution)/shard_map/while
  860.5 3.7 collective-permute-start.1
  864.2 35.2 %all-gather.9.cloned.1.call-start = ((), (), s32[]{:S(2)}) async-start(), calls=%async_computation.14 | async-start | bytes 2088960 | tf_op jit(solution)/shard_map/while/body/eval_jaxpr/all_gather | solution.py:17
  867.2 79.8 %reduce-scatter.26.cloned.1.call-start = ((), (), s32[]{:S(2)}) async-start(), calls=%async_computation.15 | async-start | bytes 2088960 | tf_op jit(solution)/shard_map/while/body/eval_jaxpr/reduce_scatter | solution.py:85
  912.4 36.0 %copy-start.2 = (bf16[272,768]{1,0:T(8,128)(2,1)S(1)}, bf16[272,768]{1,0:T(8,128)(2,1)}, u32[]{:S(2)}) copy-start(bf16[272,768]{1,0:T(8,128)(2,1)} %bitcast_select_fusion.6) | copy-start | bytes 1253380 | tf_op jit(solution)/shard_map/while
  915.2 36.1 %copy-start.29 = (s32[2,2]{1,0:T(2,128)S(1)}, s32[2,2]{1,0:T(2,128)}, u32[]{:S(2)}) copy-start(s32[2,2]{1,0:T(2,128)} %get-tuple-element.1808) | copy-start | bytes 52 | tf_op jit(solution)/shard_map/while
  915.2 67.3 %all-gather.11.cloned.1.call-start = ((), (), s32[]{:S(2)}) async-start(), calls=%async_computation.16 | async-start | bytes 2088960 | tf_op jit(solution)/shard_map/while/body/eval_jaxpr/all_gather | solution.py:17
  950.5 91.2 %reduce-scatter.36.cloned.1.call-start = ((), (), s32[]{:S(2)}) async-start(), calls=%async_computation.21 | async-start | bytes 1474560 | tf_op jit(solution)/shard_map/while/body/eval_jaxpr/reduce_scatter | solution.py:278
  964.8 79.5 %reduce-scatter.34.cloned.1.call-start = ((), (), s32[]{:S(2)}) async-start(), calls=%async_computation.20 | async-start | bytes 1474560 | tf_op jit(solution)/shard_map/while/body/eval_jaxpr/reduce_scatter | solution.py:275
  981.8 84.1 %reduce-scatter.32.cloned.1.call-start = ((), (), s32[]{:S(2)}) async-start(), calls=%async_computation.19 | async-start | bytes 491520 | tf_op jit(solution)/shard_map/while
  1024.2 68.2 %reduce-scatter.30.cloned.1.call-start = ((), (), s32[]{:S(2)}) async-start(), calls=%async_computation.18 | async-start | bytes 1228800 | tf_op jit(solution)/shard_map/while
  1036.6 89.4 %reduce-scatter.28.cloned.1.call-start = ((), (), s32[]{:S(2)}) async-start(), calls=%async_computation.17 | async-start | bytes 2088960 | tf_op jit(solution)/shard_map/while/body/eval_jaxpr/reduce_scatter | solution.py:85
  1041.7 86.0 %copy-start.3 = (bf16[272,768]{1,0:T(8,128)(2,1)S(1)}, bf16[272,768]{1,0:T(8,128)(2,1)}, u32[]{:S(2)}) copy-start(bf16[272,768]{1,0:T(8,128)(2,1)} %reduce-scatter.26.cloned.1.call-done) | copy-start | bytes 1253380 | tf_op jit(solution)/shard_map/while
  1130.0 3.7 collective-permute-start.1
  1133.7 35.2 %all-gather.9.cloned.1.call-start = ((), (), s32[]{:S(2)}) async-start(), calls=%async_computation.14 | async-start | bytes 2088960 | tf_op jit(solution)/shard_map/while/body/eval_jaxpr/all_gather | solution.py:17
  1136.8 79.8 %reduce-scatter.26.cloned.1.call-start = ((), (), s32[]{:S(2)}) async-start(), calls=%async_computation.15 | async-start | bytes 2088960 | tf_op jit(solution)/shard_map/while/body/eval_jaxpr/reduce_scatter | solution.py:85
  1184.7 36.1 %copy-start.29 = (s32[2,2]{1,0:T(2,128)S(1)}, s32[2,2]{1,0:T(2,128)}, u32[]{:S(2)}) copy-start(s32[2,2]{1,0:T(2,128)} %get-tuple-element.1808) | copy-start | bytes 52 | tf_op jit(solution)/shard_map/while
  1184.7 67.3 %all-gather.11.cloned.1.call-start = ((), (), s32[]{:S(2)}) async-start(), calls=%async_computation.16 | async-start | bytes 2088960 | tf_op jit(solution)/shard_map/while/body/eval_jaxpr/all_gather | solution.py:17
  1220.0 91.3 %reduce-scatter.36.cloned.1.call-start = ((), (), s32[]{:S(2)}) async-start(), calls=%async_computation.21 | async-start | bytes 1474560 | tf_op jit(solution)/shard_map/while/body/eval_jaxpr/reduce_scatter | solution.py:278
  1234.3 79.5 %reduce-scatter.34.cloned.1.call-start = ((), (), s32[]{:S(2)}) async-start(), calls=%async_computation.20 | async-start | bytes 1474560 | tf_op jit(solution)/shard_map/while/body/eval_jaxpr/reduce_scatter | solution.py:275
  1251.3 84.3 %reduce-scatter.32.cloned.1.call-start = ((), (), s32[]{:S(2)}) async-start(), calls=%async_computation.19 | async-start | bytes 491520 | tf_op jit(solution)/shard_map/while
  1293.8 68.5 %reduce-scatter.30.cloned.1.call-start = ((), (), s32[]{:S(2)}) async-start(), calls=%async_computation.18 | async-start | bytes 1228800 | tf_op jit(solution)/shard_map/while
  1306.1 89.6 %reduce-scatter.28.cloned.1.call-start = ((), (), s32[]{:S(2)}) async-start(), calls=%async_computation.17 | async-start | bytes 2088960 | tf_op jit(solution)/shard_map/while/body/eval_jaxpr/reduce_scatter | solution.py:85
  1311.3 86.2 %copy-start.3 = (bf16[272,768]{1,0:T(8,128)(2,1)S(1)}, bf16[272,768]{1,0:T(8,128)(2,1)}, u32[]{:S(2)}) copy-start(bf16[272,768]{1,0:T(8,128)(2,1)} %reduce-scatter.26.cloned.1.call-done) | copy-start | bytes 1253380 | tf_op jit(solution)/shard_map/while
  1399.7 3.7 collective-permute-start.1
  1403.4 126.9 %reduce-scatter.20.cloned.1.call-start = ((), (), s32[]{:S(2)}) async-start(), calls=%async_computation.9 | async-start | bytes 417792
  (88 other events, 933.8 us)
Sparse Core Ops, SparseCore 0:
  16.8 34.5 all-gather.4
  81.5 31.6 reduce-scatter.21
  117.9 31.7 all-gather.6
  164.3 31.6 reduce-scatter.23
  207.0 31.8 all-gather.4
  268.9 31.6 reduce-scatter.21
  305.2 31.7 all-gather.6
  351.6 31.6 reduce-scatter.23
  394.3 31.8 all-gather.4
  456.2 31.6 reduce-scatter.21
  492.6 31.7 all-gather.6
  539.0 31.6 reduce-scatter.23
  598.1 31.7 all-gather.8
  645.9 31.6 reduce-scatter.25
  681.3 31.7 all-gather.10
  715.4 29.1 reduce-scatter.35
  746.8 27.8 reduce-scatter.33
  777.0 19.2 reduce-scatter.31
  798.6 24.3 reduce-scatter.29
  826.2 30.2 reduce-scatter.27
  867.5 31.7 all-gather.8
  915.3 31.6 reduce-scatter.25
  950.6 31.7 all-gather.10
  984.7 29.1 reduce-scatter.35
  1016.4 27.8 reduce-scatter.33
  1046.5 19.3 reduce-scatter.31
  1068.0 24.3 reduce-scatter.29
  1095.7 30.2 reduce-scatter.27
  1137.1 31.7 all-gather.8
  1184.8 31.6 reduce-scatter.25
  1220.2 31.7 all-gather.10
  1254.4 29.1 reduce-scatter.35
  1285.9 27.8 reduce-scatter.33
  1316.2 19.2 reduce-scatter.31
  1337.9 24.3 reduce-scatter.29
  1365.4 30.2 reduce-scatter.27
Sparse Core Ops, SparseCore 1:
  1408.5 121.7 reduce-scatter.19
where the time goes:
time: 1550 us; the launch traced here: 1540 us
  waiting for transfers between devices  877 us (57%)
  matrix products  337 us (22%)
  other arithmetic  180 us (12%)
  local copies, waits for them, and re-layouts  92.9 us (6%)
  loops' own time  24.2 us (2%)
  between operations  15.7 us (1%)
    all_gather x12, waiting for transfers between devices, on_whole(): everything = lax.all_gather(slab, axis, axis=dim, tiled=True)  256 us
    reduce_scatter x6, waiting for transfers between devices, scatter_back(): lax.psum_scatter(term(jnp.int32(0), row_count * lax.axis_size('tensor'))....  189 us
    reduce_scatter x6, waiting for transfers between devices, project_scatter(): lax.psum_scatter(term(jnp.int32(0), row_count * lax.axis_size('tensor'))....  166 us
    while x42, waiting for transfers between devices  134 us
    unnamed x2, waiting for transfers between devices  124 us
    dot_general x6, matrix products, attention_scores(): jnp.einsum('qhe,khe->hqk', query, key_heads, preferred_element_type=jnp.f...  47.4 us
    dot_general x3, matrix products, section_backward(): jnp.einsum('qhe,khe->hqk', grad_mixed, head_parts[:, 2], preferred_elemen...  42.2 us
    dot_general x3, matrix products, section_backward(): jnp.einsum('sd,fd->sf', segment, down_weight, preferred_element_type=jnp....  35.7 us
  transfers between devices with their start and end apart: 43, of which 37 were waited for; matrix products, arithmetic and copies ran while one was open for 23% of the time, Pallas kernels for 0%

commit v1 on v0

v1 whole, which is shorter than its diff:
```python
import functools

import jax
import jax.numpy as jnp
from jax import lax
from jax.experimental import pallas as pl
from jax.experimental.pallas import tpu as pltpu
from jax.sharding import PartitionSpec as P

MESH = pl.DeviceIdType.MESH
VMEM = pltpu.VMEM
ANY = pl.ANY
BF = jnp.bfloat16
F32 = jnp.float32

HD = 64
WIN = 12
GRID = 24
QL = 512
EPS = 1e-05
OFF = -1e30
LIMIT = 60 * 2**20

NT = (((1,), (1,)), ((), ()))
TN = (((0,), (0,)), ((), ()))


def mm(a, b):
    return jnp.dot(a, b, preferred_element_type=F32)


def mm_nt(a, b):
    return lax.dot_general(a, b, NT, preferred_element_type=F32)


def mm_tn(a, b):
    return lax.dot_general(a, b, TN, preferred_element_type=F32)


def normalize(values):
    centered = values - jnp.mean(values, axis=-1, keepdims=True)
    inverse = lax.rsqrt(jnp.mean(centered * centered, axis=-1, keepdims=True) + EPS)
    return centered * inverse, inverse


def normalize_back(grad, normed, inverse, gain):
    t = grad * gain
    return inverse * (
        t
        - jnp.mean(t, axis=-1, keepdims=True)
        - normed * jnp.mean(t * normed, axis=-1, keepdims=True)
    )


def place():
    return lax.axis_index("section"), lax.axis_index("dp"), lax.axis_index("tensor")


def partner_of(t):
    return t + 1 - 2 * lax.rem(t, 2)


def across_of(t):
    return lax.rem(t + 2, 4)


def greet(*devices):
    barrier = pltpu.get_barrier_semaphore()
    for device in devices:
        pl.semaphore_signal(barrier, inc=1, device_id=device, device_id_type=MESH)
    pl.semaphore_wait(barrier, len(devices))


def send(src, dst, sems, index, device):
    return pltpu.make_async_remote_copy(
        src_ref=src,
        dst_ref=dst,
        send_sem=sems[0].at[index],
        recv_sem=sems[1].at[index],
        device_id=device,
        device_id_type=MESH,
    )


def pick_start(layer, refs, dsts, sem):
    core = lax.axis_index("section")

    @pl.when(core == layer)
    def _():
        for n, (mine, other) in enumerate(refs):
            pltpu.make_async_copy(mine, dsts[n], sem.at[n]).start()

    @pl.when(core != layer)
    def _():
        for n, (mine, other) in enumerate(refs):
            pltpu.make_async_copy(other, dsts[n], sem.at[n]).start()


def pick_wait(refs, dsts, sem, n):
    pltpu.make_async_copy(refs[n][0], dsts[n], sem.at[n]).wait()


def head_lanes(rows, h):
    lanes = lax.broadcasted_iota(jnp.int32, (rows, 3 * HD), 1)
    return (lanes >= h * HD) & (lanes < h * HD + HD)


def fill_bias(bias_ref, colinfo, rowinfo, rows):
    info = rowinfo[rows, :]
    cw, ca, cj = colinfo[0:1, :], colinfo[1:2, :], colinfo[2:3, :]
    rw, ra, ri = info[:, 0:1], info[:, 1:2], info[:, 2:3]
    allowed = (cw == rw) | (ca < ra) | (cj == ri)
    bias_ref[...] = jnp.where(allowed, 0.0, OFF)


def chunk_rows(i, chunk):
    return pl.ds(pl.multiple_of(i * chunk, 16), chunk)


def attn_fwd_kernel(
    layer, x_ref, gain_ref, colinfo, rowinfo, wout_ref, wa, wb, wc, wd,
    x1_ref, q_ref, k_ref, v_ref, mixed_ref, lse_ref,
    w_scr, a_scr, bias_scr, other_scr, wsem, kv_s, kv_r, mix_s, mix_r,
):
    s, d, t = place()
    partner = (s, d, partner_of(t))
    sibling = (1 - s, d, t)
    refs = [(wa, wc), (wb, wd)]
    dsts = [w_scr.at[0], w_scr.at[1]]
    pick_start(layer, refs, dsts, wsem)
    greet(partner, sibling)
    count = x_ref.shape[0]
    chunk = count // 2
    own = pl.ds(pl.multiple_of(s * count, 16), count)

    @pl.loop(0, 2)
    def _(i):
        rows = chunk_rows(i, chunk)
        normed, _ = normalize(x_ref[rows, :].astype(F32))
        a_scr[rows, :] = (normed * gain_ref[...]).astype(BF)

    for j in range(2):
        pick_wait(refs, dsts, wsem, j)
    outs = []
    for j in range(2):
        k_ref[j, own, :] = mm(a_scr[...], w_scr[j, 1]).astype(BF)
        v_ref[j, own, :] = mm(a_scr[...], w_scr[j, 2]).astype(BF)
        for n, ref in enumerate((k_ref, v_ref)):
            copy = send(ref.at[j, own], ref.at[j, own], (kv_s, kv_r), j * 2 + n, sibling)
            copy.start()
            outs.append(copy)
    for j in range(2):
        q_ref[j] = (mm(a_scr[...], w_scr[j, 0]) * HD**-0.5).astype(BF)
    for copy in outs:
        copy.wait()

    def mix_copy(i, j):
        rows = chunk_rows(i, chunk)
        return send(mixed_ref.at[j, rows], other_scr.at[j, rows], (mix_s, mix_r), i * 2 + j, partner)

    @pl.loop(0, 2)
    def _(i):
        rows = chunk_rows(i, chunk)
        fill_bias(bias_scr, colinfo, rowinfo, rows)

        @pl.loop(0, 2)
        def _(j):
            total = jnp.zeros((chunk, 3 * HD), F32)
            for h in range(3):
                lanes = head_lanes(chunk, h)
                qh = jnp.where(lanes, q_ref[j, rows, :], jnp.zeros((), BF))
                scores = mm_nt(qh, k_ref[j]) + bias_scr[...]
                top = jnp.max(scores, axis=-1, keepdims=True)
                expos = jnp.exp(scores - top)
                norm = jnp.sum(expos, axis=-1, keepdims=True)
                lse_ref[j * 3 + h, rows, :] = top + jnp.log(norm)
                probs = (expos * (1.0 / norm)).astype(BF)
                total = total + jnp.where(lanes, mm(probs, v_ref[j]), 0.0)
            mixed_ref[j, rows, :] = total.astype(BF)
            mix_copy(i, j).start()

    other = partner_of(t)

    @pl.loop(0, 2)
    def _(i):
        rows = chunk_rows(i, chunk)
        total = x_ref[rows, :].astype(F32)
        total = total + mm(mixed_ref[0, rows, :], wout_ref[t])
        total = total + mm(mixed_ref[1, rows, :], wout_ref[across_of(t)])
        for j in range(2):
            mix_copy(i, j).wait()
        total = total + mm(other_scr[0, rows, :], wout_ref[other])
        total = total + mm(other_scr[1, rows, :], wout_ref[across_of(other)])
        x1_ref[rows, :] = total


def attn_fwd(layer, cid, x, gain, colinfo, rowinfo, wout, w):
    count, width = x.shape
    tokens = colinfo.shape[1]
    part = w[0].shape[-1]
    chunk = count // 2
    dma = pltpu.SemaphoreType.DMA
    return pl.pallas_call(
        functools.partial(attn_fwd_kernel, layer),
        out_shape=(
            jax.ShapeDtypeStruct((count, width), F32),
            jax.ShapeDtypeStruct((2, count, part), BF),
            jax.ShapeDtypeStruct((2, tokens, part), BF),
            jax.ShapeDtypeStruct((2, tokens, part), BF),
            jax.ShapeDtypeStruct((2, count, part), BF),
            jax.ShapeDtypeStruct((6, count, 1), F32),
        ),
        in_specs=[pl.BlockSpec(memory_space=VMEM)] * 5 + [pl.BlockSpec(memory_space=ANY)] * 4,
        out_specs=[pl.BlockSpec(memory_space=VMEM)] * 6,
        scratch_shapes=[
            VMEM((2,) + w[0].shape, BF),
            VMEM((count, width), BF),
            VMEM((chunk, tokens), F32),
            VMEM((2, count, part), BF),
            dma((2,)),
            dma((4,)),
            dma((4,)),
            dma((4,)),
            dma((4,)),
        ],
        compiler_params=pltpu.CompilerParams(
            collective_id=cid, has_side_effects=True, vmem_limit_bytes=LIMIT
        ),
        cost_estimate=pl.CostEstimate(flops=20 * 10**9, bytes_accessed=10**7, transcendentals=0),
        name="attn_fwd%d" % layer,
    )(x, gain, colinfo, rowinfo, wout, *w)


def ffn_fwd_kernel(
    layer, x1_ref, gain_ref, ua, ub, uc, ud, da, db, dc, dd,
    y_ref, b_ref, acted_ref, slope_ref,
    up_scr, down_scr, own_scr, out_scr, in_scr, wsem, s_sem, r_sem,
):
    s, d, t = place()
    partner = (s, d, partner_of(t))
    count, width = x1_ref.shape
    units = ua.shape[1]
    refs = [(ua, uc), (ub, ud), (da, dc), (db, dd)]
    dsts = [
        up_scr.at[:, pl.ds(0, units)],
        up_scr.at[:, pl.ds(units, units)],
        down_scr.at[pl.ds(0, units)],
        down_scr.at[pl.ds(units, units)],
    ]
    pick_start(layer, refs, dsts, wsem)
    greet(partner)
    chunk = count // 2
    tile = 256

    def copy_of(i):
        rows = chunk_rows(i, chunk)
        return send(out_scr.at[rows], in_scr.at[rows], (s_sem, r_sem), i, partner)

    for n in range(4):
        pick_wait(refs, dsts, wsem, n)

    @pl.loop(0, 2)
    def _(i):
        rows = chunk_rows(i, chunk)
        normed, _ = normalize(x1_ref[rows, :])
        b_ref[rows, :] = (normed * gain_ref[...]).astype(BF)

        @pl.loop(0, 2 * units // tile)
        def _(n):
            cols = pl.ds(pl.multiple_of(n * tile, tile), tile)
            hidden = mm(b_ref[rows, :], up_scr[:, cols])
            cdf = 0.5 + 0.5 * lax.erf(hidden * 0.5**0.5)
            acted_ref[rows, cols] = (hidden * cdf).astype(BF)
            bell = jnp.exp(hidden * hidden * -0.5) * 0.3989422804014327
            slope_ref[rows, cols] = (cdf + hidden * bell).astype(BF)

        @pl.loop(0, width // tile)
        def _(n):
            cols = pl.ds(pl.multiple_of(n * tile, tile), tile)
            part = mm(acted_ref[rows, :], down_scr[:, cols])
            own_scr[rows, cols] = part
            out_scr[rows, cols] = part.astype(BF)

        copy_of(i).start()

    @pl.loop(0, 2)
    def _(i):
        rows = chunk_rows(i, chunk)
        copy_of(i).wait()
        y_ref[rows, :] = (x1_ref[rows, :] + own_scr[rows, :] + in_scr[rows, :].astype(F32)).astype(BF)


def ffn_fwd(layer, cid, x1, gain, up, down):
    count, width = x1.shape
    units = up[0].shape[1]
    dma = pltpu.SemaphoreType.DMA
    return pl.pallas_call(
        functools.partial(ffn_fwd_kernel, layer),
        out_shape=(
            jax.ShapeDtypeStruct((count, width), BF),
            jax.ShapeDtypeStruct((count, width), BF),
            jax.ShapeDtypeStruct((count, 2 * units), BF),
            jax.ShapeDtypeStruct((count, 2 * units), BF),
        ),
        in_specs=[pl.BlockSpec(memory_space=VMEM)] * 2 + [pl.BlockSpec(memory_space=ANY)] * 8,
        out_specs=[pl.BlockSpec(memory_space=VMEM)] * 4,
        scratch_shapes=[
            VMEM((width, 2 * units), BF),
            VMEM((2 * units, width), BF),
            VMEM((count, width), F32),
            VMEM((count, width), BF),
            VMEM((count, width), BF),
            dma((4,)),
            dma((2,)),
            dma((2,)),
        ],
        compiler_params=pltpu.CompilerParams(
            collective_id=cid, has_side_effects=True, vmem_limit_bytes=LIMIT
        ),
        cost_estimate=pl.CostEstimate(flops=20 * 10**9, bytes_accessed=10**7, transcendentals=0),
        name="ffn_fwd%d" % layer,
    )(x1, gain, *up, *down)


def ffn_bwd_kernel(
    layer, g_ref, x1_ref, gain_ref, b_ref, acted_ref, slope_ref, ua, ub, uc, ud, da, db, dc, dd,
    dx1_ref, dgain_ref, dup_ref, ddown_ref,
    up_scr, down_scr, own_scr, out_scr, in_scr, dh_scr, wsem, s_sem, r_sem,
):
    s, d, t = place()
    partner = (s, d, partner_of(t))
    count, width = x1_ref.shape
    units = ua.shape[1]
    refs = [(da, dc), (db, dd), (ua, uc), (ub, ud)]
    dsts = [
        down_scr.at[pl.ds(0, units)],
        down_scr.at[pl.ds(units, units)],
        up_scr.at[:, pl.ds(0, units)],
        up_scr.at[:, pl.ds(units, units)],
    ]
    pick_start(layer, refs, dsts, wsem)
    greet(partner)
    chunk = count // 2
    tile = 256

    def copy_of(i):
        rows = chunk_rows(i, chunk)
        return send(out_scr.at[rows], in_scr.at[rows], (s_sem, r_sem), i, partner)

    for n in range(4):
        pick_wait(refs, dsts, wsem, n)

    @pl.loop(0, 2)
    def _(i):
        rows = chunk_rows(i, chunk)

        @pl.loop(0, 2 * units // tile)
        def _(n):
            cols = pl.ds(pl.multiple_of(n * tile, tile), tile)
            du = mm_nt(g_ref[rows, :], down_scr[cols, :])
            dh_scr[rows, cols] = (du * slope_ref[rows, cols].astype(F32)).astype(BF)

        @pl.loop(0, width // tile)
        def _(n):
            cols = pl.ds(pl.multiple_of(n * tile, tile), tile)
            part = mm_nt(dh_scr[rows, :], up_scr[cols, :])
            own_scr[rows, cols] = part
            out_scr[rows, cols] = part.astype(BF)

        copy_of(i).start()

    for j in range(2):

        @pl.loop(0, units // tile)
        def _(n):
            here = pl.ds(pl.multiple_of(n * tile, tile), tile)
            cols = pl.ds(pl.multiple_of(n * tile, tile) + j * units, tile)
            ddown_ref[j, here, :] = mm_tn(acted_ref[:, cols], g_ref[...]).astype(BF)
            dup_ref[j, :, here] = mm_tn(b_ref[...], dh_scr[:, cols]).astype(BF)

    dgain_ref[...] = jnp.zeros_like(dgain_ref)

    @pl.loop(0, 2)
    def _(i):
        rows = chunk_rows(i, chunk)
        copy_of(i).wait()
        grad = own_scr[rows, :] + in_scr[rows, :].astype(F32)
        normed, inverse = normalize(x1_ref[rows, :])
        dgain_ref[...] += jnp.sum(grad * normed, axis=0, keepdims=True)
        dx1_ref[rows, :] = g_ref[rows, :].astype(F32) + normalize_back(
            grad, normed, inverse, gain_ref[...]
        )


def ffn_bwd(layer, cid, g, x1, gain, b, acted, slope, up, down):
    count, width = x1.shape
    units = up[0].shape[1]
    dma = pltpu.SemaphoreType.DMA
    return pl.pallas_call(
        functools.partial(ffn_bwd_kernel, layer),
        out_shape=(
            jax.ShapeDtypeStruct((count, width), F32),
            jax.ShapeDtypeStruct((1, width), F32),
            jax.ShapeDtypeStruct((2, width, units), BF),
            jax.ShapeDtypeStruct((2, units, width), BF),
        ),
        in_specs=[pl.BlockSpec(memory_space=VMEM)] * 6 + [pl.BlockSpec(memory_space=ANY)] * 8,
        out_specs=[pl.BlockSpec(memory_space=VMEM)] * 4,
        scratch_shapes=[
            VMEM((width, 2 * units), BF),
            VMEM((2 * units, width), BF),
            VMEM((count, width), F32),
            VMEM((count, width), BF),
            VMEM((count, width), BF),
            VMEM((count, 2 * units), BF),
            dma((4,)),
            dma((2,)),
            dma((2,)),
        ],
        compiler_params=pltpu.CompilerParams(
            collective_id=cid, has_side_effects=True, vmem_limit_bytes=LIMIT
        ),
        cost_estimate=pl.CostEstimate(flops=20 * 10**9, bytes_accessed=10**7, transcendentals=0),
        name="ffn_bwd%d" % layer,
    )(g, x1, gain, b, acted, slope, *up, *down)


def attn_bwd_kernel(
    layer, dx1_ref, x_ref, gain_ref, colinfo, rowinfo, wout_ref, q_ref, k_ref, v_ref, mixed_ref, lse_ref,
    wa, wb, wc, wd,
    dx_ref, dgain_ref, dqkv_ref, dout_ref,
    w_scr, a_scr, bias_scr, dc_scr, dmix_scr, dk_scr, dv_scr, dq_scr, part_scr, other_scr, d_scr,
    own_scr, out_scr, in_scr, wsem, kv_s, kv_r, s_sem, r_sem,
):
    s, d, t = place()
    partner = (s, d, partner_of(t))
    sibling = (1 - s, d, t)
    refs = [(wa, wc), (wb, wd)]
    dsts = [w_scr.at[0], w_scr.at[1]]
    pick_start(layer, refs, dsts, wsem)
    greet(partner, sibling)
    count, width = x_ref.shape
    chunk = count // 2
    tile = 256
    own = pl.ds(pl.multiple_of(s * count, 16), count)
    away = pl.ds(pl.multiple_of((1 - s) * count, 16), count)
    part = q_ref.shape[2]

    @pl.loop(0, 2)
    def _(i):
        rows = chunk_rows(i, chunk)
        normed, _ = normalize(x_ref[rows, :].astype(F32))
        a_scr[rows, :] = (normed * gain_ref[...]).astype(BF)
        dc_scr[rows, :] = dx1_ref[rows, :].astype(BF)

    dmix_scr[0] = mm_nt(dc_scr[...], wout_ref[t]).astype(BF)
    dmix_scr[1] = mm_nt(dc_scr[...], wout_ref[across_of(t)]).astype(BF)
    dk_scr[...] = jnp.zeros_like(dk_scr)
    dv_scr[...] = jnp.zeros_like(dv_scr)

    @pl.loop(0, 2)
    def _(i):
        rows = chunk_rows(i, chunk)
        fill_bias(bias_scr, colinfo, rowinfo, rows)

        @pl.loop(0, 2)
        def _(j):
            total = jnp.zeros((chunk, part), F32)
            for h in range(3):
                lanes = head_lanes(chunk, h)
                zero = jnp.zeros((), BF)
                qh = jnp.where(lanes, q_ref[j, rows, :], zero)
                dmh = jnp.where(lanes, dmix_scr[j, rows, :], zero)
                scores = mm_nt(qh, k_ref[j]) + bias_scr[...]
                probs = jnp.exp(scores - lse_ref[j * 3 + h, rows, :])
                dprobs = mm_nt(dmh, v_ref[j])
                inner = jnp.sum(probs * dprobs, axis=-1, keepdims=True)
                dscores = (probs * (dprobs - inner)).astype(BF)
                total = total + jnp.where(lanes, mm(dscores, k_ref[j]), 0.0)
                dk_scr[j] += mm_tn(dscores, qh)
                dv_scr[j] += mm_tn(probs.astype(BF), dmh)
            dq_scr[j, rows, :] = (total * HD**-0.5).astype(BF)

    part_scr[0] = dk_scr[:, away, :].astype(BF)
    part_scr[1] = dv_scr[:, away, :].astype(BF)
    copies = [send(part_scr.at[n], other_scr.at[n], (kv_s, kv_r), n, sibling) for n in range(2)]
    for copy in copies:
        copy.start()
    dout_ref[0] = mm_tn(mixed_ref[0], dc_scr[...]).astype(BF)
    dout_ref[1] = mm_tn(mixed_ref[1], dc_scr[...]).astype(BF)
    for j in range(2):
        pick_wait(refs, dsts, wsem, j)
    for copy in copies:
        copy.wait()
    d_scr[0] = dq_scr[...]
    d_scr[1] = (dk_scr[:, own, :] + other_scr[0].astype(F32)).astype(BF)
    d_scr[2] = (dv_scr[:, own, :] + other_scr[1].astype(F32)).astype(BF)

    def copy_of(i):
        rows = chunk_rows(i, chunk)
        return send(out_scr.at[rows], in_scr.at[rows], (s_sem, r_sem), i, partner)

    @pl.loop(0, 2)
    def _(i):
        rows = chunk_rows(i, chunk)

        @pl.loop(0, width // tile)
        def _(n):
            cols = pl.ds(pl.multiple_of(n * tile, tile), tile)
            total = jnp.zeros((chunk, tile), F32)
            for e in range(3):
                for j in range(2):
                    total = total + mm_nt(d_scr[e, j, rows, :], w_scr[j, e, cols, :])
            own_scr[rows, cols] = total
            out_scr[rows, cols] = total.astype(BF)

        copy_of(i).start()

    @pl.loop(0, 2)
    def _(j):
        for e in range(3):
            dqkv_ref[j, e] = mm_tn(a_scr[...], d_scr[e, j]).astype(BF)

    dgain_ref[...] = jnp.zeros_like(dgain_ref)

    @pl.loop(0, 2)
    def _(i):
        rows = chunk_rows(i, chunk)
        copy_of(i).wait()
        grad = own_scr[rows, :] + in_scr[rows, :].astype(F32)
        normed, inverse = normalize(x_ref[rows, :].astype(F32))
        dgain_ref[...] += jnp.sum(grad * normed, axis=0, keepdims=True)
        dx_ref[rows, :] = (
            dx1_ref[rows, :] + normalize_back(grad, normed, inverse, gain_ref[...])
        ).astype(BF)


def attn_bwd(layer, cid, dx1, x, gain, colinfo, rowinfo, wout, q, k, v, mixed, lse, w):
    count, width = x.shape
    tokens = colinfo.shape[1]
    part = w[0].shape[-1]
    chunk = count // 2
    dma = pltpu.SemaphoreType.DMA
    return pl.pallas_call(
        functools.partial(attn_bwd_kernel, layer),
        out_shape=(
            jax.ShapeDtypeStruct((count, width), BF),
            jax.ShapeDtypeStruct((1, width), F32),
            jax.ShapeDtypeStruct((2, 3, width, part), BF),
            jax.ShapeDtypeStruct((2, part, width), BF),
        ),
        in_specs=[pl.BlockSpec(memory_space=VMEM)] * 11 + [pl.BlockSpec(memory_space=ANY)] * 4,
        out_specs=[pl.BlockSpec(memory_space=VMEM)] * 4,
        scratch_shapes=[
            VMEM((2,) + w[0].shape, BF),
            VMEM((count, width), BF),
            VMEM((chunk, tokens), F32),
            VMEM((count, width), BF),
            VMEM((2, count, part), BF),
            VMEM((2, tokens, part), F32),
            VMEM((2, tokens, part), F32),
            VMEM((2, count, part), BF),
            VMEM((2, 2, count, part), BF),
            VMEM((2, 2, count, part), BF),
            VMEM((3, 2, count, part), BF),
            VMEM((count, width), F32),
            VMEM((count, width), BF),
            VMEM((count, width), BF),
            dma((2,)),
            dma((2,)),
            dma((2,)),
            dma((2,)),
            dma((2,)),
        ],
        compiler_params=pltpu.CompilerParams(
            collective_id=cid, has_side_effects=True, vmem_limit_bytes=LIMIT
        ),
        cost_estimate=pl.CostEstimate(flops=30 * 10**9, bytes_accessed=10**7, transcendentals=0),
        name="attn_bwd%d" % layer,
    )(dx1, x, gain, colinfo, rowinfo, wout, q, k, v, mixed, lse, *w)


BOTH = ("section", "tensor")


def route(block, pairs):
    return lax.ppermute(block, BOTH, pairs)


def after(block, *others):
    return lax.optimization_barrier((block,) + others)[0]


def token_info(size, length, offsets, core, count):
    patches = GRID * GRID
    tokens = jnp.arange(patches + QL, dtype=jnp.int32)
    is_patch = tokens < patches
    row, col = tokens // GRID, tokens % GRID
    live_patch = is_patch & (row < size[0]) & (col < size[1])
    live_answer = jnp.logical_not(is_patch) & (tokens - patches < length)
    window = (row + offsets[0]) // WIN * 8 + (col + offsets[1]) // WIN
    cw = jnp.where(live_patch, window, -1)
    ca = jnp.where(live_patch, -1, jnp.where(live_answer, tokens, 1 << 20))
    colinfo = jnp.stack([cw, ca, tokens] + [tokens] * 5)
    rw = jnp.where(is_patch, window, -2)
    ra = jnp.where(is_patch, -5, tokens)
    rowinfo = jnp.stack([rw, ra, tokens], axis=1)
    return colinfo, lax.dynamic_slice_in_dim(rowinfo, core * count, count, 0)


def on_device(inputs, cotangent, w_qkv, w_out, w_up, w_down, gains, image_sizes, lengths, shifts):
    core = lax.axis_index("section")
    t = lax.axis_index("tensor")
    dp = lax.axis_size("dp")
    pair = t // 2
    quarter, width = inputs.shape[1], inputs.shape[2]
    count = 2 * quarter

    def images_in(block):
        def one(i, j):
            pairs = [(k * 4 + 2 * c + j, c * 4 + 2 * i + k) for c in range(2) for k in range(2)]
            return route(block[i], pairs)

        parts = [jnp.where(pair == 0, one(0, j), one(1, j)) for j in range(2)]
        return jnp.concatenate(parts, axis=0)

    def images_out(rows, section):
        mine = lax.dynamic_slice_in_dim(rows, lax.rem(t, 2) * quarter, quarter, 0)
        return [
            route(mine, [(c * 4 + 2 * i + m, section * 4 + 2 * c + m) for c in range(2) for m in range(2)])
            for i in range(2)
        ]

    across = [[(c * 4 + i, c * 4 + (i + 2) % 4) for i in range(4)] for c in range(2)]
    cores = [(i, (i + 4) % 8) for i in range(8)]

    def fetch(block, anchor=None):
        if anchor is not None:
            block = after(block, anchor)
        far = route(block, across[0] + across[1])
        return [block, far, route(block, cores), route(far, cores)]

    x = images_in(inputs)
    qkv_ws = fetch(w_qkv[0])
    every_out = lax.all_gather(w_out[0], "tensor", axis=0)
    every_out = lax.all_gather(every_out, "section", axis=0)
    gain_all = lax.all_gather(gains[0], "section", axis=0)
    up_ws = fetch(w_up[0])
    down_ws = fetch(w_down[0])
    cot = images_in(cotangent)

    size = lax.dynamic_index_in_dim(image_sizes, pair, 0, keepdims=False)
    length = lax.dynamic_index_in_dim(lengths, pair, 0, keepdims=False)

    kept = []
    for layer in range(2):
        info = token_info(size, length, shifts * layer, core, count)
        one, two = gain_all[layer, 0][None], gain_all[layer, 1][None]
        x1, q, k, v, mixed, lse = attn_fwd(layer, layer, x, one, *info, every_out[layer], qkv_ws)
        y, b, acted, slope = ffn_fwd(layer, 2 + layer, x1, two, up_ws, down_ws)
        kept.append((x, x1, q, k, v, mixed, lse, b, acted, slope, info, one, two))
        x = y

    out_y = images_out(y, 1)

    def reduce_weights(layer, grad, dim):
        own, far = grad[0], grad[1]
        here, there = layer, 1 - layer
        far = far + route(far, [(here * 4 + i, there * 4 + i) for i in range(4)])
        own_more = route(own, [(there * 4 + i, here * 4 + i) for i in range(4)])
        far_more = route(far, [(there * 4 + i, here * 4 + (i + 2) % 4) for i in range(4)])
        total = own + own_more + far_more
        return lax.psum_scatter(total, "dp", scatter_dimension=dim, tiled=True).astype(F32)

    g = cot
    grads = [None, None]
    gain_grads = [None, None]
    for layer in (1, 0):
        x, x1, q, k, v, mixed, lse, b, acted, slope, info, one, two = kept[layer]
        dx1, dtwo, dup, ddown = ffn_bwd(layer, 4 + layer, g, x1, two, b, acted, slope, up_ws, down_ws)
        g_up = reduce_weights(layer, dup, 0)
        g_down = reduce_weights(layer, ddown, 0)
        g, done, dqkv, dout = attn_bwd(
            layer, 6 + layer, dx1, x, one, *info, every_out[layer], q, k, v, mixed, lse, qkv_ws
        )
        g_qkv = reduce_weights(layer, dqkv, 1)
        g_out = reduce_weights(layer, dout, 1)
        grads[layer] = (g_qkv, g_out, g_up, g_down)
        gain_grads[layer] = jnp.concatenate([done, dtwo], axis=0)

    out_g = images_out(g, 0)
    ends = jnp.stack([jnp.where(core == 0, a, b) for a, b in zip(out_g, out_y)])
    shares = [jnp.where(core == 0, a, b)[None] for a, b in zip(*grads)]
    gain_total = lax.psum(jnp.stack(gain_grads) * 0.5, ("section", "dp", "tensor"))
    mine = lax.dynamic_index_in_dim(gain_total, core, 0, keepdims=True)
    share = width // (dp * 4)
    slot = lax.axis_index("dp") * 4 + t
    gain_share = lax.dynamic_slice_in_dim(mine, slot * share, share, 2)
    return (ends[None], *shares, gain_share)


def solution(mesh):
    placed = (
        P("dp", "tensor", None),
        P("dp", "tensor", None),
        P("section", None, None, "tensor"),
        P("section", "tensor", None),
        P("section", None, "tensor"),
        P("section", "tensor", None),
        P("section", None, None),
        P("dp", None),
        P("dp"),
        P(),
    )
    return jax.shard_map(
        on_device,
        mesh=mesh,
        in_specs=placed,
        out_specs=(
            P("section", "dp", "tensor", None),
            P("section", None, "dp", "tensor"),
            P("section", "tensor", "dp"),
            P("section", "dp", "tensor"),
            P("section", ("tensor", "dp"), None),
            P("section", None, ("dp", "tensor")),
        ),
        check_vma=False,
    )
```

time: 1550 us -> 696 us (0.45)
  waiting for transfers between devices: 877 us -> 122 us
  matrix products: 337 us -> 0 us
  Pallas kernels: 0 us -> 279 us
  other arithmetic: 180 us -> 42.7 us
  starting transfers between devices: 12.8 us -> 127 us
  blocking collectives: 0 us -> 45.7 us
  local copies, waits for them, and re-layouts: 92.9 us -> 59.3 us
  loops' own time: 24.2 us -> 0 us
    reduce_scatter x18 -> x6, waiting for transfers between devices: 357 us -> 26.3 us  [reduce_weights(): lax.psum_scatter(total, 'dp', scatter_dimension=dim, tiled=True).astype(F32)]
    dot_general x54 -> x0, matrix products: 328 us -> none  [the longest x6 47.4 us: attention_scores(): jnp.einsum('qhe,khe->hqk', query, key_heads, preferred_element_type=jnp.f...]
    pallas_call x0 -> x8, Pallas kernels: none -> 279 us  [the longest x2 106 us: attn_bwd(): pl.pallas_call(functools.partial(attn_bwd_kernel, layer), out_shape=(jax....]
    all_gather x12 -> x2, waiting for transfers between devices: 256 us -> 27 us  [the longest x1 27 us: on_device(): every_out = lax.all_gather(w_out[0], 'tensor', axis=0)]
    while x42 -> x0, waiting for transfers between devices: 134 us -> none
    unnamed x2 -> x12, waiting for transfers between devices: 124 us -> 0.85 us
    ppermute x6 -> x45, starting transfers between devices: 11.4 us -> 127 us  [route(): return lax.ppermute(block, BOTH, pairs)]
    ppermute x6 -> x45, waiting for transfers between devices: 6.33 us -> 68.1 us  [route(): return lax.ppermute(block, BOTH, pairs)]
  transfers between devices with their start and end apart: 43 -> 55, of which waited for: 37 -> 12; matrix products, arithmetic and copies ran while one was open for 23% -> 14% of each run, Pallas kernels for 0% -> 4%
where the time goes in v1:
time: 696 us; the launch traced here: 692 us
  Pallas kernels  279 us (40%)
  starting transfers between devices  127 us (18%)
  waiting for transfers between devices  122 us (18%)
  local copies, waits for them, and re-layouts  59.3 us (9%)
  blocking collectives  45.7 us (7%)
  other arithmetic  42.7 us (6%)
  between operations  15.6 us (2%)
    ppermute x45, starting transfers between devices, route(): return lax.ppermute(block, BOTH, pairs)  127 us
    pallas_call x2, Pallas kernels, attn_bwd(): pl.pallas_call(functools.partial(attn_bwd_kernel, layer), out_shape=(jax....  106 us
    ppermute x45, waiting for transfers between devices, route(): return lax.ppermute(block, BOTH, pairs)  68.1 us
    pallas_call x2, Pallas kernels, ffn_bwd(): pl.pallas_call(functools.partial(ffn_bwd_kernel, layer), out_shape=(jax.S...  61.1 us
    pallas_call x2, Pallas kernels, ffn_fwd(): pl.pallas_call(functools.partial(ffn_fwd_kernel, layer), out_shape=(jax.S...  58.7 us
    pallas_call x2, Pallas kernels, attn_fwd(): pl.pallas_call(functools.partial(attn_fwd_kernel, layer), out_shape=(jax....  52.3 us
    psum x1, blocking collectives, on_device(): lax.psum(jnp.stack(gain_grads) * 0.5, ('section', 'dp', 'tensor'))  43.9 us
    all_gather x1, waiting for transfers between devices, on_device(): every_out = lax.all_gather(w_out[0], 'tensor', axis=0)  27 us
  transfers between devices with their start and end apart: 55, of which 12 were waited for; matrix products, arithmetic and copies ran while one was open for 14% of the time, Pallas kernels for 4%

profile of v1, /device:TPU:0, one launch (start us, length us, event | category | flops | bytes accessed | tf_op | source)
XLA Modules:
  0.0 691.7 jit_solution(3560194931464768527)
XLA Ops:
  8.0 2.1 slice_bitcast_fusion.12
  11.5 4.7 collective-permute-start.5
  17.6 1.7 collective-permute-start.4
  19.2 3.6 collective-permute-start.8
  25.1 27.0 %all-gather.4.cloned.1.call-done = bf16[4,192,768]{2,1,0:T(8,128)(2,1)} async-done(((bf16[1,192,768]{2,1,0:T(8,128)(2,1)}), bf16[4,192,768]{2,1,0:T(8,128)(2,1)}) %all-gather.4.cloned.1.call-update) | async-done | bytes 1179664 | tf_op jit(solution)/shard_map/all_gather | solution.py:645
  56.6 1.9 fusion.7
  60.8 2.6 add_select_fusion
  64.2 1.8 all_gather.12
  66.0 2.8 collective-permute-start.1
  70.8 2.0 collective-permute-start.14
  73.9 1.9 collective-permute-done.1
  75.8 1.7 collective-permute-start
  79.0 2.3 collective-permute-start.9
  83.5 50.4 %collective-permute-start.12 = (bf16[768,768]{1,0:T(8,128)(2,1)}, bf16[768,768]{1,0:T(8,128)(2,1)}, u32[]{:S(2)}, u32[]{:S(2)}) collective-permute-start(bf16[768,768]{1,0:T(8,128)(2,1)} %bitcast.15.ua), channel_id=1, source_target_pairs={{0,16},{1,17},{2,18},{3,19},{16,0},{17,1},{18,2},{19,3},{4,20},{5,... | collective-permute-start | bytes 3538952 | tf_op jit(solution)/shard_map/ppermute | solution.py:587
  134.9 1.9 copy.50.wb
  140.2 3.2 fusion.16
  143.5 26.1 %attn_fwd0.1 = (f32[544,768]{1,0:T(8,128)}, bf16[2,544,192]{2,1,0:T(8,128)(2,1)}, bf16[2,1088,192]{2,1,0:T(8,128)(2,1)}, bf16[2,1088,192]{2,1,0:T(8,128)(2,1)}, ...) custom-call(bf16[544,768]{1,0:T(8,128)(2,1)} %pad_maximum_fusion.1.x_ref, f32[1,768]{1,0:T(1,128)} %get-tuple-element.103.gain_ref, ...), custom_call_target="tpu_custom_call" | custom-call | flops 20000000000 | bytes 10000000 | tf_op jit(solution)/shard_map/attn_fwd0/pallas_call | solution.py:203
  169.6 29.2 %ffn_fwd0.1 = (bf16[544,768]{1,0:T(8,128)(2,1)}, bf16[544,768]{1,0:T(8,128)(2,1)}, bf16[544,1536]{1,0:T(8,128)(2,1)}, bf16[544,1536]{1,0:T(8,128)(2,1)}) custom-call(f32[544,768]{1,0:T(8,128)} %get-tuple-element.42.x1_ref, f32[1,768]{1,0:T(1,128)} %get-tuple-element.102.gain_ref, bf16[768,768]{1,0:T(8,128)(2,1)} %bitcast.15.ua, ...), custom_call_target="tpu_custom_call" | custom-call | flops 20000000000 | bytes 10000000 | tf_op jit(solution)/shard_map/ffn_fwd0/pallas_call | solution.py:297
  198.8 26.2 %attn_fwd1.1 = (f32[544,768]{1,0:T(8,128)}, bf16[2,544,192]{2,1,0:T(8,128)(2,1)}, bf16[2,1088,192]{2,1,0:T(8,128)(2,1)}, bf16[2,1088,192]{2,1,0:T(8,128)(2,1)}, ...) custom-call(bf16[544,768]{1,0:T(8,128)(2,1)} %get-tuple-element.43.x_ref, f32[1,768]{1,0:T(1,128)} %get-tuple-element.101.gain_ref, ...), custom_call_target="tpu_custom_call" | custom-call | flops 20000000000 | bytes 10000000 | tf_op jit(solution)/shard_map/attn_fwd1/pallas_call | solution.py:203
  225.0 29.5 %ffn_fwd1.1 = (bf16[544,768]{1,0:T(8,128)(2,1)}, bf16[544,768]{1,0:T(8,128)(2,1)}, bf16[544,1536]{1,0:T(8,128)(2,1)}, bf16[544,1536]{1,0:T(8,128)(2,1)}) custom-call(f32[544,768]{1,0:T(8,128)} %get-tuple-element.44.x1_ref, f32[1,768]{1,0:T(1,128)} %get-tuple-element.100.gain_ref, bf16[768,768]{1,0:T(8,128)(2,1)} %bitcast.15.ua, ...), custom_call_target="tpu_custom_call" | custom-call | flops 20000000000 | bytes 10000000 | tf_op jit(solution)/shard_map/ffn_fwd1/pallas_call | solution.py:297
  254.5 30.2 %ffn_bwd1.1 = (f32[544,768]{1,0:T(8,128)}, f32[1,768]{1,0:T(1,128)}, bf16[2,768,768]{2,1,0:T(8,128)(2,1)}, bf16[2,768,768]{2,1,0:T(8,128)(2,1)}) custom-call(bf16[544,768]{1,0:T(8,128)(2,1)} %pad_maximum_fusion.g_ref, f32[544,768]{1,0:T(8,128)} %get-tuple-element.44.x1_ref, f32[1,768]{1,0:T(1,128)} %get-tuple-element.100.gain_ref, ...), custom_call_target="tpu_custom_call" | custom-call | flops 20000000000 | bytes 10000000 | tf_op jit(solution)/shard_map/ffn_bwd1/pallas_call | solution.py:399
  284.7 53.3 %attn_bwd1.1 = (bf16[544,768]{1,0:T(8,128)(2,1)}, f32[1,768]{1,0:T(1,128)}, bf16[2,3,768,192]{3,2,1,0:T(8,128)(2,1)}, bf16[2,192,768]{2,1,0:T(8,128)(2,1)}) custom-call(f32[544,768]{1,0:T(8,128)} %get-tuple-element.48.dx1_ref, bf16[544,768]{1,0:T(8,128)(2,1)} %get-tuple-element.43.x_ref, f32[1,768]{1,0:T(1,128)} %get-tuple-element.101.gain_ref, ...), custom_call_target="tpu_custom_call" | custom-call | flops 30000001024 | bytes 10000000 | tf_op jit(solution)/shard_map/attn_bwd1/pallas_call | solution.py:544
  338.1 31.0 %ffn_bwd0.1 = (f32[544,768]{1,0:T(8,128)}, f32[1,768]{1,0:T(1,128)}, bf16[2,768,768]{2,1,0:T(8,128)(2,1)}, bf16[2,768,768]{2,1,0:T(8,128)(2,1)}) custom-call(bf16[544,768]{1,0:T(8,128)(2,1)} %get-tuple-element.54.g_ref, f32[544,768]{1,0:T(8,128)} %get-tuple-element.42.x1_ref, f32[1,768]{1,0:T(1,128)} %get-tuple-element.102.gain_ref, ...), custom_call_target="tpu_custom_call" | custom-call | flops 20000000000 | bytes 10000000 | tf_op jit(solution)/shard_map/ffn_bwd0/pallas_call | solution.py:399
  369.0 53.2 %attn_bwd0.1 = (bf16[544,768]{1,0:T(8,128)(2,1)}, f32[1,768]{1,0:T(1,128)}, bf16[2,3,768,192]{3,2,1,0:T(8,128)(2,1)}, bf16[2,192,768]{2,1,0:T(8,128)(2,1)}) custom-call(f32[544,768]{1,0:T(8,128)} %get-tuple-element.58.dx1_ref, bf16[544,768]{1,0:T(8,128)(2,1)} %pad_maximum_fusion.1.x_ref, f32[1,768]{1,0:T(1,128)} %get-tuple-element.103.gain_ref, ...), custom_call_target="tpu_custom_call" | custom-call | flops 30000001024 | bytes 10000000 | tf_op jit(solution)/shard_map/attn_bwd0/pallas_call | solution.py:544
  422.2 1.9 slice_bitcast_fusion.19
  425.4 4.5 collective-permute-start.28
  429.9 1.8 slice_bitcast_fusion.11
  433.1 2.2 collective-permute-start.22
  436.1 2.0 collective-permute-start.30
  439.4 1.6 copy.63
  441.1 1.8 fusion.8
  448.0 3.2 collective-permute-done.29
  454.6 1.7 copy.66
  457.6 2.4 copy.67
  462.3 5.7 collective-permute-start.32
  468.1 7.4 %collective-permute-done.32 = bf16[192,768]{1,0:T(8,128)(2,1)S(1)} collective-permute-done((bf16[192,768]{1,0:T(8,128)(2,1)S(1)}, bf16[192,768]{1,0:T(8,128)(2,1)S(1)}, u32[]{:S(2)}, u32[]{:S(2)}) %collective-permute-start.32) | collective-permute-done | bytes 294944 | tf_op jit(solution)/shard_map/ppermute | solution.py:587
  475.5 1.8 add_add_fusion.6
  477.3 1.9 copy.77
  480.7 4.4 collective-permute-start.24
  485.1 2.4 copy.64
  489.0 2.3 copy.68
  491.4 3.0 add_add_fusion.5
  494.4 2.7 fusion.11
  497.1 2.3 copy.73
  499.4 2.2 collective-permute-start.26
  503.1 2.3 collective-permute-start.34
  506.7 1.7 copy.70
  508.4 3.1 collective-permute-done.26
  511.5 2.3 copy.74
  513.8 2.6 add_add_fusion.4
  516.5 1.9 fusion.12
  519.8 1.6 slice_bitcast_fusion.5
  522.7 13.3 %collective-permute-done.35 = bf16[768,768]{1,0:T(8,128)(2,1)S(1)} collective-permute-done((bf16[768,768]{1,0:T(8,128)(2,1)S(1)}, bf16[768,768]{1,0:T(8,128)(2,1)S(1)}, u32[]{:S(2)}, u32[]{:S(2)}) %collective-permute-start.35) | collective-permute-done | bytes 1179680 | tf_op jit(solution)/shard_map/ppermute | solution.py:587
  536.0 2.5 add_add_fusion.3
  541.5 1.6 slice_bitcast_fusion.3
  544.6 10.6 %collective-permute-done.38 = bf16[768,768]{1,0:T(8,128)(2,1)S(1)} collective-permute-done((bf16[768,768]{1,0:T(8,128)(2,1)S(1)}, bf16[768,768]{1,0:T(8,128)(2,1)S(1)}, u32[]{:S(2)}, u32[]{:S(2)}) %collective-permute-start.38) | collective-permute-done | bytes 1179680 | tf_op jit(solution)/shard_map/ppermute | solution.py:587
  563.6 13.3 %collective-permute-done.41 = bf16[768,768]{1,0:T(8,128)(2,1)S(1)} collective-permute-done((bf16[768,768]{1,0:T(8,128)(2,1)S(1)}, bf16[768,768]{1,0:T(8,128)(2,1)S(1)}, u32[]{:S(2)}, u32[]{:S(2)}) %collective-permute-start.41) | collective-permute-done | bytes 1179680 | tf_op jit(solution)/shard_map/ppermute | solution.py:587
  582.2 12.5 %collective-permute-done.44 = bf16[768,768]{1,0:T(8,128)(2,1)S(1)} collective-permute-done((bf16[768,768]{1,0:T(8,128)(2,1)S(1)}, bf16[768,768]{1,0:T(8,128)(2,1)S(1)}, u32[]{:S(2)}, u32[]{:S(2)}) %collective-permute-start.44) | collective-permute-done | bytes 1179680 | tf_op jit(solution)/shard_map/ppermute | solution.py:587
  597.9 3.9 collective-permute-start.18
  603.9 43.9 %psum.7 = f32[2,2,768]{2,1,0:T(2,128)S(1)} all-reduce(f32[2,2,768]{2,1,0:T(2,128)S(1)} %maximum_multiply_fusion), channel_id=1, replica_groups=mesh['section'=2,'dp'=4,'tensor'=4] {'section','dp','tensor'}, use_global_device_ids=true, to_apply=%region_8.9 | all-reduce | flops 3072 | bytes 24576 | tf_op jit(solution)/shard_map/psum | solution.py:694
  652.3 1.9 select_bitcast_fusion.2
  654.2 1.9 select_bitcast_fusion.1
  656.2 26.3 %reduce-scatter.23.cloned.1.call-done = bf16[192,768]{1,0:T(8,128)(2,1)} async-done(((bf16[768,768]{1,0:T(8,128)(2,1)}), bf16[192,768]{1,0:T(8,128)(2,1)}) %reduce-scatter.23.cloned.1.call-update) | async-done | bytes 294928 | tf_op jit(solution)/shard_map/reduce_scatter | solution.py:673
  682.5 1.9 select_bitcast_fusion
  (208 shorter events, 77.2 us)
Async XLA Ops:
  7.2 45.0 %copy-start = (s32[2,2]{1,0:T(2,128)S(1)}, s32[2,2]{1,0:T(2,128)}, u32[]{:S(2)}) copy-start(s32[2,2]{1,0:T(2,128)} %param.17) | copy-start | bytes 52
  7.2 12.1 %copy-start.15 = (bf16[1,3,768,192]{2,3,1,0:T(8,128)(2,1)S(1)}, bf16[1,3,768,192]{2,3,1,0:T(8,128)(2,1)}, u32[]{:S(2)}) copy-start(bf16[1,3,768,192]{2,3,1,0:T(8,128)(2,1)} %param.12) | copy-start | bytes 2654212
  7.2 15.7 %copy-start.28 = (s32[2]{0:T(128)S(1)}, s32[2]{0:T(128)}, u32[]{:S(2)}) copy-start(s32[2]{0:T(128)} %param.19) | copy-start | bytes 28
  7.2 44.8 %all-gather.4.cloned.1.call-start = ((), (), s32[]{:S(2)}) async-start(), calls=%async_computation.8 | async-start | bytes 1474560 | tf_op jit(solution)/shard_map/all_gather | solution.py:645
  7.9 132.3 %all-gather.6.cloned.1.call-start = ((), (), s32[]{:S(2)}) async-start(), calls=%async_computation.15 | async-start | bytes 3538944 | tf_op jit(solution)/shard_map/all_gather | solution.py:646
  10.1 50.1 %collective-permute-start.7 = (bf16[272,768]{1,0:T(8,128)(2,1)}, bf16[272,768]{1,0:T(8,128)(2,1)}, u32[]{:S(2)}, u32[]{:S(2)}) collective-permute-start(bf16[272,768]{1,0:T(8,128)(2,1)} %get-tuple-element.92), channel_id=1, source_target_pairs={{1,2},{17,3},{3,18},{19,19},{5,6},{21,7},{7,22},{23,23},{9,10},{25... | collective-permute-start | bytes 1253384 | tf_op jit(solution)/shard_map/ppermute | solution.py:587
  11.5 54.4 %collective-permute-start.5 = (bf16[272,768]{1,0:T(8,128)(2,1)}, bf16[272,768]{1,0:T(8,128)(2,1)S(1)}, u32[]{:S(2)}, u32[]{:S(2)}) collective-permute-start(bf16[272,768]{1,0:T(8,128)(2,1)} %get-tuple-element.92), channel_id=1, source_target_pairs={{0,2},{16,3},{2,18},{18,19},{4,6},{20,7},{6,22},{22,23},{8,10},{24... | collective-permute-start | bytes 1253384 | tf_op jit(solution)/shard_map/ppermute | solution.py:587
  16.3 52.6 %collective-permute-start.6 = (bf16[272,768]{1,0:T(8,128)(2,1)}, bf16[272,768]{1,0:T(8,128)(2,1)}, u32[]{:S(2)}, u32[]{:S(2)}) collective-permute-start(bf16[272,768]{1,0:T(8,128)(2,1)} %get-tuple-element.93), channel_id=1, source_target_pairs={{1,0},{17,1},{3,16},{19,17},{5,4},{21,5},{7,20},{23,21},{9,8},{25,... | collective-permute-start | bytes 1253384 | tf_op jit(solution)/shard_map/ppermute | solution.py:587
  17.6 53.2 %collective-permute-start.4 = (bf16[272,768]{1,0:T(8,128)(2,1)}, bf16[272,768]{1,0:T(8,128)(2,1)S(1)}, u32[]{:S(2)}, u32[]{:S(2)}) collective-permute-start(bf16[272,768]{1,0:T(8,128)(2,1)} %get-tuple-element.93), channel_id=1, source_target_pairs={{0,0},{16,1},{2,16},{18,17},{4,4},{20,5},{6,20},{22,21},{8,8},{24,... | collective-permute-start | bytes 1253384 | tf_op jit(solution)/shard_map/ppermute | solution.py:587
  19.2 62.1 %collective-permute-start.8 = (bf16[3,768,192]{1,2,0:T(8,128)(2,1)S(1)}, bf16[3,768,192]{1,2,0:T(8,128)(2,1)S(1)}, u32[]{:S(2)}, u32[]{:S(2)}) collective-permute-start(bf16[3,768,192]{1,2,0:T(8,128)(2,1)S(1)} %bitcast.117), channel_id=1, source_target_pairs={{0,2},{1,3},{2,0},{3,1},{16,18},{17,19},{18,16},{19,17},{4,6},{5,7... | collective-permute-start | bytes 2654216 | tf_op jit(solution)/shard_map/ppermute | solution.py:587
  52.1 597.5 %reduce-scatter.25.cloned.1.call-start = ((), (), s32[]{:S(2)}) async-start(), calls=%async_computation.16 | async-start | bytes 491520
  60.2 10.7 %collective-permute-start.3 = (bf16[272,768]{1,0:T(8,128)(2,1)}, bf16[272,768]{1,0:T(8,128)(2,1)S(1)}, u32[]{:S(2)}, u32[]{:S(2)}) collective-permute-start(bf16[272,768]{1,0:T(8,128)(2,1)} %get-tuple-element.94), channel_id=1, source_target_pairs={{1,2},{17,3},{3,18},{19,19},{5,6},{21,7},{7,22},{23,23},{9,10},{25... | collective-permute-start | bytes 1253384 | tf_op jit(solution)/shard_map/ppermute | solution.py:587
  66.0 11.5 %copy-start.17 = (bf16[272,768]{1,0:T(8,128)(2,1)}, bf16[272,768]{1,0:T(8,128)(2,1)S(1)}, u32[]{:S(2)}) copy-start(bf16[272,768]{1,0:T(8,128)(2,1)S(1)} %collective-permute-done.5) | copy-start | bytes 1253380
  66.0 9.9 %collective-permute-start.1 = (bf16[272,768]{1,0:T(8,128)(2,1)}, bf16[272,768]{1,0:T(8,128)(2,1)S(1)}, u32[]{:S(2)}, u32[]{:S(2)}) collective-permute-start(bf16[272,768]{1,0:T(8,128)(2,1)} %get-tuple-element.94), channel_id=1, source_target_pairs={{0,2},{16,3},{2,18},{18,19},{4,6},{20,7},{6,22},{22,23},{8,10},{24... | collective-permute-start | bytes 1253384 | tf_op jit(solution)/shard_map/ppermute | solution.py:587
  68.8 10.1 %collective-permute-start.2 = (bf16[272,768]{1,0:T(8,128)(2,1)}, bf16[272,768]{1,0:T(8,128)(2,1)S(1)}, u32[]{:S(2)}, u32[]{:S(2)}) collective-permute-start(bf16[272,768]{1,0:T(8,128)(2,1)} %get-tuple-element.95), channel_id=1, source_target_pairs={{1,0},{17,1},{3,16},{19,17},{5,4},{21,5},{7,20},{23,21},{9,8},{25,... | collective-permute-start | bytes 1253384 | tf_op jit(solution)/shard_map/ppermute | solution.py:587
  70.7 67.5 %collective-permute-start.11 = (bf16[768,768]{1,0:T(8,128)(2,1)}, bf16[768,768]{1,0:T(8,128)(2,1)}, u32[]{:S(2)}, u32[]{:S(2)}) collective-permute-start(bf16[768,768]{1,0:T(8,128)(2,1)} %bitcast.15.ua), channel_id=1, source_target_pairs={{0,2},{1,3},{2,0},{3,1},{16,18},{17,19},{18,16},{19,17},{4,6},{5,7... | collective-permute-start | bytes 3538952 | tf_op jit(solution)/shard_map/ppermute | solution.py:587
  70.8 10.5 %copy-start.19 = (bf16[272,768]{1,0:T(8,128)(2,1)}, bf16[272,768]{1,0:T(8,128)(2,1)S(1)}, u32[]{:S(2)}) copy-start(bf16[272,768]{1,0:T(8,128)(2,1)S(1)} %collective-permute-done.3) | copy-start | bytes 1253380
  70.8 67.9 %collective-permute-start.14 = (bf16[768,768]{1,0:T(8,128)(2,1)}, bf16[768,768]{1,0:T(8,128)(2,1)}, u32[]{:S(2)}, u32[]{:S(2)}) collective-permute-start(bf16[768,768]{1,0:T(8,128)(2,1)} %bitcast.121), channel_id=1, source_target_pairs={{0,2},{1,3},{2,0},{3,1},{16,18},{17,19},{18,16},{19,17},{4,6},{5,7... | collective-permute-start | bytes 3538952 | tf_op jit(solution)/shard_map/ppermute | solution.py:587
  75.8 7.7 %collective-permute-start = (bf16[272,768]{1,0:T(8,128)(2,1)}, bf16[272,768]{1,0:T(8,128)(2,1)S(1)}, u32[]{:S(2)}, u32[]{:S(2)}) collective-permute-start(bf16[272,768]{1,0:T(8,128)(2,1)} %get-tuple-element.95), channel_id=1, source_target_pairs={{0,0},{16,1},{2,16},{18,17},{4,4},{20,5},{6,20},{22,21},{8,8},{24,... | collective-permute-start | bytes 1253384 | tf_op jit(solution)/shard_map/ppermute | solution.py:587
  79.0 57.8 %collective-permute-start.9 = (bf16[3,768,192]{1,2,0:T(8,128)(2,1)S(1)}, bf16[3,768,192]{1,2,0:T(8,128)(2,1)S(1)}, u32[]{:S(2)}, u32[]{:S(2)}) collective-permute-start(bf16[3,768,192]{1,2,0:T(8,128)(2,1)S(1)} %bitcast.118), channel_id=1, source_target_pairs={{0,16},{1,17},{2,18},{3,19},{16,0},{17,1},{18,2},{19,3},{4,20},{5,... | collective-permute-start | bytes 2654216 | tf_op jit(solution)/shard_map/ppermute | solution.py:587
  81.3 57.5 %collective-permute-start.10 = (bf16[3,768,192]{1,2,0:T(8,128)(2,1)S(1)}, bf16[3,768,192]{1,2,0:T(8,128)(2,1)S(1)}, u32[]{:S(2)}, u32[]{:S(2)}) collective-permute-start(bf16[3,768,192]{1,2,0:T(8,128)(2,1)S(1)} %collective-permute-done.8), channel_id=1, source_target_pairs={{0,16},{1,17},{2,18},{3,19},{16,0},{17,1},{18,2},{19,3},{4,20},{5,... | collective-permute-start | bytes 2654216 | tf_op jit(solution)/shard_map/ppermute | solution.py:587
  83.5 86.0 %collective-permute-start.12 = (bf16[768,768]{1,0:T(8,128)(2,1)}, bf16[768,768]{1,0:T(8,128)(2,1)}, u32[]{:S(2)}, u32[]{:S(2)}) collective-permute-start(bf16[768,768]{1,0:T(8,128)(2,1)} %bitcast.15.ua), channel_id=1, source_target_pairs={{0,16},{1,17},{2,18},{3,19},{16,0},{17,1},{18,2},{19,3},{4,20},{5,... | collective-permute-start | bytes 3538952 | tf_op jit(solution)/shard_map/ppermute | solution.py:587
  136.8 32.7 %collective-permute-start.15 = (bf16[768,768]{1,0:T(8,128)(2,1)}, bf16[768,768]{1,0:T(8,128)(2,1)}, u32[]{:S(2)}, u32[]{:S(2)}) collective-permute-start(bf16[768,768]{1,0:T(8,128)(2,1)} %bitcast.122), channel_id=1, source_target_pairs={{0,16},{1,17},{2,18},{3,19},{16,0},{17,1},{18,2},{19,3},{4,20},{5,... | collective-permute-start | bytes 3538952 | tf_op jit(solution)/shard_map/ppermute | solution.py:587
  138.2 31.3 %collective-permute-start.13 = (bf16[768,768]{1,0:T(8,128)(2,1)}, bf16[768,768]{1,0:T(8,128)(2,1)}, u32[]{:S(2)}, u32[]{:S(2)}) collective-permute-start(bf16[768,768]{1,0:T(8,128)(2,1)} %collective-permute-done.11.ub), channel_id=1, source_target_pairs={{0,16},{1,17},{2,18},{3,19},{16,0},{17,1},{18,2},{19,3},{4,20},{5,... | collective-permute-start | bytes 3538952 | tf_op jit(solution)/shard_map/ppermute | solution.py:587
  138.8 30.8 %collective-permute-start.16 = (bf16[768,768]{1,0:T(8,128)(2,1)}, bf16[768,768]{1,0:T(8,128)(2,1)}, u32[]{:S(2)}, u32[]{:S(2)}) collective-permute-start(bf16[768,768]{1,0:T(8,128)(2,1)} %collective-permute-done.14.db), channel_id=1, source_target_pairs={{0,16},{1,17},{2,18},{3,19},{16,0},{17,1},{18,2},{19,3},{4,20},{5,... | collective-permute-start | bytes 3538952 | tf_op jit(solution)/shard_map/ppermute | solution.py:587
  424.1 22.6 %collective-permute-start.27 = (bf16[192,768]{1,0:T(8,128)(2,1)}, bf16[192,768]{1,0:T(8,128)(2,1)}, u32[]{:S(2)}, u32[]{:S(2)}) collective-permute-start(bf16[192,768]{1,0:T(8,128)(2,1)} %get-tuple-element.96), channel_id=1, source_target_pairs={{16,0},{17,1},{18,2},{19,3},{20,4},{21,5},{22,6},{23,7},{24,8},{25... | collective-permute-start | bytes 884744 | tf_op jit(solution)/shard_map/ppermute | solution.py:587
  425.4 15.7 %collective-permute-start.28 = (bf16[192,768]{1,0:T(8,128)(2,1)}, bf16[192,768]{1,0:T(8,128)(2,1)}, u32[]{:S(2)}, u32[]{:S(2)}) collective-permute-start(bf16[192,768]{1,0:T(8,128)(2,1)} %get-tuple-element.97), channel_id=1, source_target_pairs={{0,16},{1,17},{2,18},{3,19},{4,20},{5,21},{6,22},{7,23},{8,24},{9,... | collective-permute-start | bytes 884744 | tf_op jit(solution)/shard_map/ppermute | solution.py:587
  433.1 21.6 %collective-permute-start.22 = (bf16[3,768,192]{1,2,0:T(8,128)(2,1)}, bf16[3,768,192]{1,2,0:T(8,128)(2,1)}, u32[]{:S(2)}, u32[]{:S(2)}) collective-permute-start(bf16[3,768,192]{1,2,0:T(8,128)(2,1)} %copy.65), channel_id=1, source_target_pairs={{0,16},{1,17},{2,18},{3,19},{4,20},{5,21},{6,22},{7,23},{8,24},{9,... | collective-permute-start | bytes 2654216 | tf_op jit(solution)/shard_map/ppermute | solution.py:587
  436.1 31.9 %collective-permute-start.30 = (bf16[192,768]{1,0:T(8,128)(2,1)}, bf16[192,768]{1,0:T(8,128)(2,1)}, u32[]{:S(2)}, u32[]{:S(2)}) collective-permute-start(bf16[192,768]{1,0:T(8,128)(2,1)} %get-tuple-element.98), channel_id=1, source_target_pairs={{0,16},{1,17},{2,18},{3,19},{4,20},{5,21},{6,22},{7,23},{8,24},{9,... | collective-permute-start | bytes 884744 | tf_op jit(solution)/shard_map/ppermute | solution.py:587
  438.1 23.2 %collective-permute-start.31 = (bf16[192,768]{1,0:T(8,128)(2,1)}, bf16[192,768]{1,0:T(8,128)(2,1)}, u32[]{:S(2)}, u32[]{:S(2)}) collective-permute-start(bf16[192,768]{1,0:T(8,128)(2,1)} %get-tuple-element.99), channel_id=1, source_target_pairs={{16,0},{17,1},{18,2},{19,3},{20,4},{21,5},{22,6},{23,7},{24,8},{25... | collective-permute-start | bytes 884744 | tf_op jit(solution)/shard_map/ppermute | solution.py:587
  442.9 8.3 %collective-permute-start.29 = (bf16[192,768]{1,0:T(8,128)(2,1)}, bf16[192,768]{1,0:T(8,128)(2,1)}, u32[]{:S(2)}, u32[]{:S(2)}) collective-permute-start(bf16[192,768]{1,0:T(8,128)(2,1)} %fusion.8), channel_id=1, source_target_pairs={{16,2},{17,3},{18,0},{19,1},{20,6},{21,7},{22,4},{23,5},{24,10},{2... | collective-permute-start | bytes 884744 | tf_op jit(solution)/shard_map/ppermute | solution.py:587
  446.7 38.4 %collective-permute-start.21 = (bf16[3,768,192]{1,2,0:T(8,128)(2,1)}, bf16[3,768,192]{1,2,0:T(8,128)(2,1)}, u32[]{:S(2)}, u32[]{:S(2)}) collective-permute-start(bf16[3,768,192]{1,2,0:T(8,128)(2,1)} %copy.63), channel_id=1, source_target_pairs={{16,0},{17,1},{18,2},{19,3},{20,4},{21,5},{22,6},{23,7},{24,8},{25... | collective-permute-start | bytes 2654216 | tf_op jit(solution)/shard_map/ppermute | solution.py:587
  451.2 36.3 %collective-permute-start.25 = (bf16[3,768,192]{1,2,0:T(8,128)(2,1)}, bf16[3,768,192]{1,2,0:T(8,128)(2,1)}, u32[]{:S(2)}, u32[]{:S(2)}) collective-permute-start(bf16[3,768,192]{1,2,0:T(8,128)(2,1)} %copy.71), channel_id=1, source_target_pairs={{16,0},{17,1},{18,2},{19,3},{20,4},{21,5},{22,6},{23,7},{24,8},{25... | collective-permute-start | bytes 2654216 | tf_op jit(solution)/shard_map/ppermute | solution.py:587
  454.6 196.0 %reduce-scatter.27.cloned.1.call-start = ((), (), s32[]{:S(2)}) async-start(), calls=%async_computation.17 | async-start | bytes 491520
  460.0 29.0 %collective-permute-start.23 = (bf16[3,768,192]{1,2,0:T(8,128)(2,1)}, bf16[3,768,192]{1,2,0:T(8,128)(2,1)}, u32[]{:S(2)}, u32[]{:S(2)}) collective-permute-start(bf16[3,768,192]{1,2,0:T(8,128)(2,1)} %copy.67), channel_id=1, source_target_pairs={{16,2},{17,3},{18,0},{19,1},{20,6},{21,7},{22,4},{23,5},{24,10},{2... | collective-permute-start | bytes 2654216 | tf_op jit(solution)/shard_map/ppermute | solution.py:587
  462.3 17.0 %copy-start.11 = (bf16[3,768,192]{2,1,0:T(8,128)(2,1)S(1)}, bf16[3,768,192]{2,1,0:T(8,128)(2,1)}, u32[]{:S(2)}) copy-start(bf16[3,768,192]{2,1,0:T(8,128)(2,1)} %get-tuple-element.88) | copy-start | bytes 2654212
  462.3 13.1 %collective-permute-start.32 = (bf16[192,768]{1,0:T(8,128)(2,1)S(1)}, bf16[192,768]{1,0:T(8,128)(2,1)S(1)}, u32[]{:S(2)}, u32[]{:S(2)}) collective-permute-start(bf16[192,768]{1,0:T(8,128)(2,1)S(1)} %fusion.9), channel_id=1, source_target_pairs={{0,18},{1,19},{2,16},{3,17},{4,22},{5,23},{6,20},{7,21},{8,26},{9,... | collective-permute-start | bytes 884744 | tf_op jit(solution)/shard_map/ppermute | solution.py:587
  479.2 173.1 %reduce-scatter.13.cloned.1.call-start = ((), (), s32[]{:S(2)}) async-start(), calls=%async_computation.9 | async-start | bytes 1474560 | tf_op jit(solution)/shard_map/reduce_scatter | solution.py:673
  480.7 26.1 %collective-permute-start.24 = (bf16[3,768,192]{1,2,0:T(8,128)(2,1)}, bf16[3,768,192]{1,2,0:T(8,128)(2,1)}, u32[]{:S(2)}, u32[]{:S(2)}) collective-permute-start(bf16[3,768,192]{1,2,0:T(8,128)(2,1)} %copy.69), channel_id=1, source_target_pairs={{0,16},{1,17},{2,18},{3,19},{4,20},{5,21},{6,22},{7,23},{8,24},{9,... | collective-permute-start | bytes 2654216 | tf_op jit(solution)/shard_map/ppermute | solution.py:587
  494.3 157.9 %reduce-scatter.15.cloned.1.call-start = ((), (), s32[]{:S(2)}) async-start(), calls=%async_computation.10 | async-start | bytes 1474560 | tf_op jit(solution)/shard_map/reduce_scatter | solution.py:673
  499.4 12.1 %collective-permute-start.26 = (bf16[3,768,192]{1,2,0:T(8,128)(2,1)}, bf16[3,768,192]{1,2,0:T(8,128)(2,1)}, u32[]{:S(2)}, u32[]{:S(2)}) collective-permute-start(bf16[3,768,192]{1,2,0:T(8,128)(2,1)} %copy.73), channel_id=1, source_target_pairs={{0,18},{1,19},{2,16},{3,17},{4,22},{5,23},{6,20},{7,21},{8,26},{9,... | collective-permute-start | bytes 2654216 | tf_op jit(solution)/shard_map/ppermute | solution.py:587
  503.1 13.4 %collective-permute-start.34 = (bf16[768,768]{1,0:T(8,128)(2,1)}, bf16[768,768]{1,0:T(8,128)(2,1)}, u32[]{:S(2)}, u32[]{:S(2)}) collective-permute-start(bf16[768,768]{1,0:T(8,128)(2,1)} %get-tuple-element.83), channel_id=1, source_target_pairs={{0,16},{1,17},{2,18},{3,19},{4,20},{5,21},{6,22},{7,23},{8,24},{9,... | collective-permute-start | bytes 3538952 | tf_op jit(solution)/shard_map/ppermute | solution.py:587
  505.4 17.2 %collective-permute-start.33 = (bf16[768,768]{1,0:T(8,128)(2,1)}, bf16[768,768]{1,0:T(8,128)(2,1)}, u32[]{:S(2)}, u32[]{:S(2)}) collective-permute-start(bf16[768,768]{1,0:T(8,128)(2,1)} %get-tuple-element.82), channel_id=1, source_target_pairs={{16,0},{17,1},{18,2},{19,3},{20,4},{21,5},{22,6},{23,7},{24,8},{25... | collective-permute-start | bytes 3538952 | tf_op jit(solution)/shard_map/ppermute | solution.py:587
  516.5 137.8 %reduce-scatter.17.cloned.1.call-start = ((), (), s32[]{:S(2)}) async-start(), calls=%async_computation.11 | async-start | bytes 1474560 | tf_op jit(solution)/shard_map/reduce_scatter | solution.py:673
  518.5 17.5 %collective-permute-start.35 = (bf16[768,768]{1,0:T(8,128)(2,1)S(1)}, bf16[768,768]{1,0:T(8,128)(2,1)S(1)}, u32[]{:S(2)}, u32[]{:S(2)}) collective-permute-start(bf16[768,768]{1,0:T(8,128)(2,1)S(1)} %fusion.12), channel_id=1, source_target_pairs={{16,2},{17,3},{18,0},{19,1},{20,6},{21,7},{22,4},{23,5},{24,10},{2... | collective-permute-start | bytes 3538952 | tf_op jit(solution)/shard_map/ppermute | solution.py:587
  519.8 16.2 %copy-start.7 = (bf16[2,768,768]{2,1,0:T(8,128)(2,1)S(1)}, bf16[2,768,768]{2,1,0:T(8,128)(2,1)}, u32[]{:S(2)}) copy-start(bf16[2,768,768]{2,1,0:T(8,128)(2,1)} %get-tuple-element.70) | copy-start | bytes 7077892
  521.4 18.6 %collective-permute-start.37 = (bf16[768,768]{1,0:T(8,128)(2,1)}, bf16[768,768]{1,0:T(8,128)(2,1)S(1)}, u32[]{:S(2)}, u32[]{:S(2)}) collective-permute-start(bf16[768,768]{1,0:T(8,128)(2,1)} %get-tuple-element.85), channel_id=1, source_target_pairs={{16,0},{17,1},{18,2},{19,3},{20,4},{21,5},{22,6},{23,7},{24,8},{25... | collective-permute-start | bytes 3538952 | tf_op jit(solution)/shard_map/ppermute | solution.py:587
  538.5 115.8 %reduce-scatter.19.cloned.1.call-start = ((), (), s32[]{:S(2)}) async-start(), calls=%async_computation.12 | async-start | bytes 1474560 | tf_op jit(solution)/shard_map/reduce_scatter | solution.py:673
  538.5 6.0 collective-permute-start.36
  540.2 15.0 %collective-permute-start.38 = (bf16[768,768]{1,0:T(8,128)(2,1)S(1)}, bf16[768,768]{1,0:T(8,128)(2,1)S(1)}, u32[]{:S(2)}, u32[]{:S(2)}) collective-permute-start(bf16[768,768]{1,0:T(8,128)(2,1)S(1)} %fusion.13), channel_id=1, source_target_pairs={{0,18},{1,19},{2,16},{3,17},{4,22},{5,23},{6,20},{7,21},{8,26},{9,... | collective-permute-start | bytes 3538952 | tf_op jit(solution)/shard_map/ppermute | solution.py:587
  543.2 14.8 %collective-permute-start.40 = (bf16[768,768]{1,0:T(8,128)(2,1)}, bf16[768,768]{1,0:T(8,128)(2,1)S(1)}, u32[]{:S(2)}, u32[]{:S(2)}) collective-permute-start(bf16[768,768]{1,0:T(8,128)(2,1)} %get-tuple-element.79), channel_id=1, source_target_pairs={{0,16},{1,17},{2,18},{3,19},{4,20},{5,21},{6,22},{7,23},{8,24},{9,... | collective-permute-start | bytes 3538952 | tf_op jit(solution)/shard_map/ppermute | solution.py:587
  556.4 99.7 %reduce-scatter.21.cloned.1.call-start = ((), (), s32[]{:S(2)}) async-start(), calls=%async_computation.13 | async-start | bytes 1474560 | tf_op jit(solution)/shard_map/reduce_scatter | solution.py:673
  556.5 7.1 %collective-permute-start.39 = (bf16[768,768]{1,0:T(8,128)(2,1)}, bf16[768,768]{1,0:T(8,128)(2,1)S(1)}, u32[]{:S(2)}, u32[]{:S(2)}) collective-permute-start(bf16[768,768]{1,0:T(8,128)(2,1)} %get-tuple-element.78), channel_id=1, source_target_pairs={{16,0},{17,1},{18,2},{19,3},{20,4},{21,5},{22,6},{23,7},{24,8},{25... | collective-permute-start | bytes 3538952 | tf_op jit(solution)/shard_map/ppermute | solution.py:587
  559.4 17.5 %collective-permute-start.41 = (bf16[768,768]{1,0:T(8,128)(2,1)S(1)}, bf16[768,768]{1,0:T(8,128)(2,1)S(1)}, u32[]{:S(2)}, u32[]{:S(2)}) collective-permute-start(bf16[768,768]{1,0:T(8,128)(2,1)S(1)} %fusion.14), channel_id=1, source_target_pairs={{16,2},{17,3},{18,0},{19,1},{20,6},{21,7},{22,4},{23,5},{24,10},{2... | collective-permute-start | bytes 3538952 | tf_op jit(solution)/shard_map/ppermute | solution.py:587
  560.7 16.2 %copy-start.4 = (bf16[2,768,768]{2,1,0:T(8,128)(2,1)S(1)}, bf16[2,768,768]{2,1,0:T(8,128)(2,1)}, u32[]{:S(2)}) copy-start(bf16[2,768,768]{2,1,0:T(8,128)(2,1)} %get-tuple-element.72) | copy-start | bytes 7077892
  562.3 17.3 %collective-permute-start.43 = (bf16[768,768]{1,0:T(8,128)(2,1)}, bf16[768,768]{1,0:T(8,128)(2,1)S(1)}, u32[]{:S(2)}, u32[]{:S(2)}) collective-permute-start(bf16[768,768]{1,0:T(8,128)(2,1)} %get-tuple-element.81), channel_id=1, source_target_pairs={{16,0},{17,1},{18,2},{19,3},{20,4},{21,5},{22,6},{23,7},{24,8},{25... | collective-permute-start | bytes 3538952 | tf_op jit(solution)/shard_map/ppermute | solution.py:587
  578.2 104.3 %reduce-scatter.23.cloned.1.call-start = ((), (), s32[]{:S(2)}) async-start(), calls=%async_computation.14 | async-start | bytes 1474560 | tf_op jit(solution)/shard_map/reduce_scatter | solution.py:673
  578.2 4.0 collective-permute-start.42
  579.8 15.0 %collective-permute-start.44 = (bf16[768,768]{1,0:T(8,128)(2,1)S(1)}, bf16[768,768]{1,0:T(8,128)(2,1)S(1)}, u32[]{:S(2)}, u32[]{:S(2)}) collective-permute-start(bf16[768,768]{1,0:T(8,128)(2,1)S(1)} %fusion.15), channel_id=1, source_target_pairs={{0,18},{1,19},{2,16},{3,17},{4,22},{5,23},{6,20},{7,21},{8,26},{9,... | collective-permute-start | bytes 3538952 | tf_op jit(solution)/shard_map/ppermute | solution.py:587
  597.2 51.3 %collective-permute-start.20 = (bf16[272,768]{1,0:T(8,128)(2,1)S(1)}, bf16[272,768]{1,0:T(8,128)(2,1)S(1)}, u32[]{:S(2)}, u32[]{:S(2)}) collective-permute-start(bf16[272,768]{1,0:T(8,128)(2,1)S(1)} %constant_dynamic-slice_fusion.1), channel_id=1, source_target_pairs={{2,16},{3,17},{18,18},{19,19},{6,20},{7,21},{22,22},{23,23},{10,24... | collective-permute-start | bytes 1253384 | tf_op jit(solution)/shard_map/ppermute | solution.py:587
  597.9 50.7 %collective-permute-start.18 = (bf16[272,768]{1,0:T(8,128)(2,1)S(1)}, bf16[272,768]{1,0:T(8,128)(2,1)S(1)}, u32[]{:S(2)}, u32[]{:S(2)}) collective-permute-start(bf16[272,768]{1,0:T(8,128)(2,1)S(1)} %constant_dynamic-slice_fusion.1), channel_id=1, source_target_pairs={{0,16},{1,17},{16,18},{17,19},{4,20},{5,21},{20,22},{21,23},{8,24}... | collective-permute-start | bytes 1253384 | tf_op jit(solution)/shard_map/ppermute | solution.py:587
  601.8 46.6 %collective-permute-start.19 = (bf16[272,768]{1,0:T(8,128)(2,1)S(1)}, bf16[272,768]{1,0:T(8,128)(2,1)S(1)}, u32[]{:S(2)}, u32[]{:S(2)}) collective-permute-start(bf16[272,768]{1,0:T(8,128)(2,1)S(1)} %constant_dynamic-slice_fusion.2), channel_id=1, source_target_pairs={{2,0},{3,1},{18,2},{19,3},{6,4},{7,5},{22,6},{23,7},{10,8},{11,9},... | collective-permute-start | bytes 1253384 | tf_op jit(solution)/shard_map/ppermute | solution.py:587
  603.1 45.4 %collective-permute-start.17 = (bf16[272,768]{1,0:T(8,128)(2,1)S(1)}, bf16[272,768]{1,0:T(8,128)(2,1)S(1)}, u32[]{:S(2)}, u32[]{:S(2)}) collective-permute-start(bf16[272,768]{1,0:T(8,128)(2,1)S(1)} %constant_dynamic-slice_fusion.2), channel_id=1, source_target_pairs={{0,0},{1,1},{16,2},{17,3},{4,4},{5,5},{20,6},{21,7},{8,8},{9,9},{2... | collective-permute-start | bytes 1253384 | tf_op jit(solution)/shard_map/ppermute | solution.py:587
  652.3 32.1 %copy-start.1 = (s32[2,2]{1,0:T(2,128)S(1)}, s32[2,2]{1,0:T(2,128)}, u32[]{:S(2)}) copy-start(s32[2,2]{1,0:T(2,128)} %param.17) | copy-start | bytes 52
  (21 other events, 111.7 us)
Sparse Core Ops, SparseCore 0:
  9.9 42.1 all-gather.3
  53.6 10.9 all-gather.5
  454.7 22.5 reduce-scatter.24
  480.2 21.3 reduce-scatter.26
  503.7 27.4 reduce-scatter.12
  533.3 27.8 reduce-scatter.14
  563.6 27.8 reduce-scatter.16
  593.8 27.8 reduce-scatter.18
  624.1 28.2 reduce-scatter.20
  654.5 27.9 reduce-scatter.22
